TPU v7x, 512 devices: a whole 4x4x16 slice. The times are simulated.
512 devices in a mesh: dp: 16 (over y, x_hi, core), seq: 16 (over z), kv: 2 (over x_lo).
Axes of the slice: x: 4 (x_hi: 2, x_lo: 2; x = x_hi * 2 + x_lo), y: 4, z: 16, core: 2. Of those that a mesh axis runs over, the one named last changes fastest.
Arguments:
- slab_queries: bfloat16 [16, 768, 1152], P('dp', 'seq'), may hold values from -16 to 16
- key_tokens: bfloat16 [16, 8192, 1152], P('dp', ('seq', 'kv')), may hold values from -16 to 16
- value_tokens: bfloat16 [16, 8192, 1152], P('dp', ('seq', 'kv')), may hold values from -6 to 6
- grad_output: bfloat16 [16, 768, 1152], P('dp'), may hold values from -6 to 6
- out_weight: bfloat16 [1152, 1152], P('seq'), may hold values from -0.1875 to 0.1875
Outputs:
- grad_keys: bfloat16 [16, 8192, 1152], P('dp', ('seq', 'kv'))
- grad_values: bfloat16 [16, 8192, 1152], P('dp', ('seq', 'kv'))
- grad_queries: bfloat16 [16, 768, 1152], P('dp', ('seq', 'kv'))
- grad_weight: float32 [1152, 1152], P('seq', ('dp', 'kv'))
All inputs are finite; a program needn't handle non-finite values.
Results may differ from a plain program's by a relative error of at most 0.02.
Values may be sent and summed in bfloat16 or wider, within the bound.
No kernel may reach another device: no remote copies, remote signals or barrier semaphores. Data moves between devices by JAX's collectives and lax.ppermute only.
A program may use at most 128 MiB of HBM per device.

v0:
```python
import math

import jax
import jax.numpy as jnp
from jax import lax
from jax.sharding import PartitionSpec as P

HEADS = 16


def combined_all(value, axis, join):
    pieces = jax.tree.map(lambda part: lax.all_gather(part, axis), value)
    head = jax.tree.map(lambda part: part[0], pieces)
    tail = jax.tree.map(lambda part: part[1:], pieces)
    so_far, _ = lax.scan(lambda so_far, section: (join(so_far, section), None), head, tail)
    return so_far


def combine(earlier, latter):
    highest = jnp.maximum(earlier[0], latter[0])
    weight_one = jnp.exp(earlier[0] - highest)
    weight_two = jnp.exp(latter[0] - highest)
    return (
        highest,
        earlier[1] * weight_one + latter[1] * weight_two,
        earlier[2] * weight_one + latter[2] * weight_two,
    )


def attention_grads(query_all, key_all, value_all, grad_heads, head_count, reduce_stats):
    row_count = query_all.shape[0]
    key_count = key_all.shape[0]
    width = query_all.shape[1] // head_count
    factor = 1.0 / math.sqrt(width)
    block_size = math.gcd(key_count, max(1, 1024 // head_count))
    blocks = key_count // block_size
    query_heads = query_all.reshape(row_count, head_count, width)
    grad_split = grad_heads.reshape(row_count, head_count, width)
    key_blocks = key_all.reshape(blocks, block_size, head_count, width)
    value_blocks = value_all.reshape(blocks, block_size, head_count, width)

    def scores_of(key_part, value_part):
        logits = (
            jnp.einsum("rhd,nhd->hrn", query_heads, key_part, preferred_element_type=jnp.float32)
            * factor
        )
        upstream = jnp.einsum(
            "rhd,nhd->hrn", grad_split, value_part, preferred_element_type=jnp.float32
        )
        return (logits, upstream)

    def first_pass(running, pieces):
        logits, upstream = scores_of(pieces[0], pieces[1])
        highest = jnp.maximum(running[0], jnp.max(logits, axis=2))
        rescale = jnp.exp(running[0] - highest)
        weights = jnp.exp(logits - highest[:, :, None])
        totals = running[1] * rescale + jnp.sum(weights, axis=2)
        weighted = running[2] * rescale + jnp.sum(weights * upstream, axis=2)
        return ((highest, totals, weighted), None)

    zeros_stat = jnp.zeros((head_count, row_count), jnp.float32)
    start_stats = (jnp.full((head_count, row_count), -1e30, jnp.float32), zeros_stat, zeros_stat)
    statistics, unused = lax.scan(first_pass, start_stats, (key_blocks, value_blocks))
    highest, totals, weighted = reduce_stats(statistics)
    delta_rows = weighted / totals

    def second_pass(running, pieces):
        logits, upstream = scores_of(pieces[0], pieces[1])
        probabilities = jnp.exp(logits - highest[:, :, None]) / totals[:, :, None]
        probs_low = probabilities.astype(jnp.bfloat16)
        grad_scores = (probabilities * (upstream - delta_rows[:, :, None])).astype(jnp.bfloat16)
        query_sum = (
            running[0]
            + jnp.einsum("hrn,nhd->rhd", grad_scores, pieces[0], preferred_element_type=jnp.float32)
            * factor
        )
        output_sum = running[1] + jnp.einsum(
            "hrn,nhd->rhd", probs_low, pieces[1], preferred_element_type=jnp.float32
        )
        grad_value = jnp.einsum(
            "hrn,rhd->nhd", probs_low, grad_split, preferred_element_type=jnp.float32
        ).astype(jnp.bfloat16)
        grad_key = (
            jnp.einsum("hrn,rhd->nhd", grad_scores, query_heads, preferred_element_type=jnp.float32)
            * factor
        ).astype(jnp.bfloat16)
        return ((query_sum, output_sum), (grad_key, grad_value))

    zeros_rows = jnp.zeros((row_count, head_count, width), jnp.float32)
    sums, outputs = lax.scan(second_pass, (zeros_rows, zeros_rows), (key_blocks, value_blocks))
    query_grad = sums[0].reshape(row_count, head_count * width)
    attn_part = sums[1].reshape(row_count, head_count * width)
    key_grad = outputs[0].reshape(key_count, head_count * width)
    value_grad = outputs[1].reshape(key_count, head_count * width)
    return (query_grad, attn_part, key_grad, value_grad)


def on_device(slab_queries, key_tokens, value_tokens, grad_output, out_weight):
    query_rows = slab_queries[0]
    key_rows = key_tokens[0]
    value_rows = value_tokens[0]
    cotangent = grad_output[0]
    grad_cols = lax.dot_general(
        cotangent, out_weight, (((1,), (1,)), ((), ())), preferred_element_type=jnp.float32
    ).astype(jnp.bfloat16)
    query_heads, key_heads, value_heads = (
        lax.all_to_all(query_rows, "seq", split_axis=1, concat_axis=0, tiled=True),
        lax.all_to_all(key_rows, "seq", split_axis=1, concat_axis=0, tiled=True),
        lax.all_to_all(value_rows, "seq", split_axis=1, concat_axis=0, tiled=True),
    )

    def reduce_pair(statistics):
        return combined_all(statistics, "kv", combine)

    local_heads = HEADS // lax.axis_size("seq")
    query_grad, attn_part, key_grad, value_grad = attention_grads(
        query_heads, key_heads, value_heads, grad_cols, local_heads, reduce_pair
    )
    key_out, value_out = (
        lax.all_to_all(key_grad, "seq", split_axis=0, concat_axis=1, tiled=True),
        lax.all_to_all(value_grad, "seq", split_axis=0, concat_axis=1, tiled=True),
    )
    query_back = lax.all_to_all(query_grad, "seq", split_axis=0, concat_axis=1, tiled=True)
    query_out = lax.psum_scatter(query_back, "kv", scatter_dimension=0, tiled=True)
    cotangent_wide = cotangent.astype(jnp.float32)
    weight_part = lax.psum_scatter(
        lax.dot_general(
            cotangent_wide,
            attn_part,
            (((0,), (0,)), ((), ())),
            precision=lax.Precision.HIGHEST,
            preferred_element_type=jnp.float32,
        ).astype(jnp.bfloat16),
        ("dp", "kv"),
        scatter_dimension=0,
        tiled=True,
    ).astype(jnp.float32)
    return (key_out[None], value_out[None], query_out.astype(jnp.bfloat16)[None], weight_part.T)


def solution(mesh):
    placed = (
        P("dp", "seq", None),
        P("dp", ("seq", "kv"), None),
        P("dp", ("seq", "kv"), None),
        P("dp", None, None),
        P("seq", None),
    )
    return jax.shard_map(
        on_device,
        mesh=mesh,
        in_specs=placed,
        out_specs=(
            P("dp", ("seq", "kv"), None),
            P("dp", ("seq", "kv"), None),
            P("dp", ("seq", "kv"), None),
            P("seq", ("dp", "kv")),
        ),
        check_vma=False,
    )
```

profile of v0, /device:TPU:1, one launch (start us, length us, event | category | flops | bytes accessed | tf_op | source)
XLA Modules:
  0.0 392.2 jit_solution(15241423309819979156)
XLA Ops:
  8.0 1.4 all_to_all.77
  10.1 15.9 %all-to-all-start.1 = ((bf16[48,16,72]{2,0,1:T(8,128)(2,1)}), bf16[48,16,72]{2,0,1:T(8,128)(2,1)S(1)}, u32[]{:S(2)}, u32[]{:S(2)}) async-start(bf16[48,16,72]{2,0,1:T(8,128)(2,1)} %copy.57), calls=%async_computation.1 | async-start | bytes 393216 | tf_op jit(solution)/shard_map/all_to_all | solution.py:107
  26.0 2.1 copy.55
  28.1 10.4 %all-to-all-done.1 = bf16[48,16,72]{2,0,1:T(8,128)(2,1)S(1)} async-done(((bf16[48,16,72]{2,0,1:T(8,128)(2,1)}), bf16[48,16,72]{2,0,1:T(8,128)(2,1)S(1)}, u32[]{:S(2)}, u32[]{:S(2)}) %all-to-all-start.1) | async-done | bytes 110624 | tf_op jit(solution)/shard_map/all_to_all | solution.py:107
  38.6 8.8 %all-to-all-start = ((bf16[256,16,72]{0,2,1:T(8,128)(2,1)}), bf16[256,16,72]{0,2,1:T(8,128)(2,1)S(1)}, u32[]{:S(2)}, u32[]{:S(2)}) async-start(bf16[256,16,72]{0,2,1:T(8,128)(2,1)} %bitcast), calls=%async_computation | async-start | bytes 1179648 | tf_op jit(solution)/shard_map/all_to_all | solution.py:108
  48.5 24.2 %all-to-all-done = bf16[256,16,72]{0,2,1:T(8,128)(2,1)S(1)} async-done(((bf16[256,16,72]{0,2,1:T(8,128)(2,1)}), bf16[256,16,72]{0,2,1:T(8,128)(2,1)S(1)}, u32[]{:S(2)}, u32[]{:S(2)}) %all-to-all-start) | async-done | bytes 589856 | tf_op jit(solution)/shard_map/all_to_all | solution.py:108
  72.7 13.1 %all-to-all-start.2 = ((bf16[256,16,72]{0,2,1:T(8,128)(2,1)}), bf16[256,16,72]{0,2,1:T(8,128)(2,1)}, u32[]{:S(2)}, u32[]{:S(2)}) async-start(bf16[256,16,72]{0,2,1:T(8,128)(2,1)} %bitcast.5), calls=%async_computation.2 | async-start | bytes 1179648 | tf_op jit(solution)/shard_map/all_to_all | solution.py:109
  87.7 1.7 reshape.282
  90.4 20.7 %all-to-all-done.2 = bf16[256,16,72]{0,2,1:T(8,128)(2,1)} async-done(((bf16[256,16,72]{0,2,1:T(8,128)(2,1)}), bf16[256,16,72]{0,2,1:T(8,128)(2,1)}, u32[]{:S(2)}, u32[]{:S(2)}) %all-to-all-start.2) | async-done | bytes 589856 | tf_op jit(solution)/shard_map/all_to_all | solution.py:109
  114.6 12.0 %while.38 = (s32[]{:T(128)}, f32[1,768]{1,0:T(1,128)S(1)}, f32[1,768]{1,0:T(1,128)S(1)}, f32[1,768]{1,0:T(1,128)S(1)}, bf16[4,1024,1,72]{1,3,2,0:T(8,128)(2,1)},...) while((s32[]{:T(128)}, f32[1,768]{1,0:T(1,128)S(1)}, ...), condition=%wide.region_4.5_spmd.clone, body=%wide.region_0.4_spmd.clone.sunk | while | flops 233575680 | bytes 10012800 | solution.py:63
  114.6 1.5 multiply_reduce_fusion.4
  117.6 1.5 multiply_reduce_fusion.4
  120.6 1.5 multiply_reduce_fusion.4
  123.6 1.5 multiply_reduce_fusion.4
  126.6 3.2 all-gather.3
  129.7 3.2 all-gather.5
  132.9 3.2 all-gather.4
  136.1 26.9 %while.39 = (s32[]{:T(128)}, f32[768,1,72]{0,2,1:T(8,128)S(1)}, f32[768,1,72]{0,2,1:T(8,128)S(1)}, bf16[4,1024,1,72]{1,3,2,0:T(8,128)(2,1)}, bf16[4,1024,1,72]{1...) while((s32[]{:T(128)}, f32[768,1,72]{0,2,1:T(8,128)S(1)}, ...), condition=%wide.region_6.7_spmd.clone, body=%wide.region_5.6_spmd.clone.sunk | while | flops 686266368 | bytes 19542212 | solution.py:90
  136.2 1.7 exponential_divide_fusion.2
  138.3 1.3 fusion.106
  140.2 1.3 fusion.103
  141.6 1.3 fusion.105
  142.9 1.7 exponential_divide_fusion.2
  145.0 1.3 fusion.106
  147.0 1.3 fusion.103
  148.3 1.3 fusion.105
  149.6 1.7 exponential_divide_fusion.2
  151.8 1.3 fusion.106
  153.7 1.3 fusion.103
  155.0 1.3 fusion.105
  156.3 1.7 exponential_divide_fusion.2
  158.5 1.3 fusion.106
  160.4 1.3 fusion.103
  161.7 1.3 fusion.105
  163.9 13.1 %all-to-all-start.5 = ((f32[16,48,72]{2,1,0:T(8,128)}), f32[16,48,72]{2,1,0:T(8,128)S(1)}, u32[]{:S(2)}, u32[]{:S(2)}) async-start(f32[16,48,72]{2,1,0:T(8,128)} %bitcast.22), calls=%async_computation.5 | async-start | bytes 786432 | tf_op jit(solution)/shard_map/all_to_all | solution.py:123
  177.0 1.5 copy.68
  179.7 2.1 copy.69
  181.8 9.9 %all-to-all-done.5 = f32[16,48,72]{2,1,0:T(8,128)S(1)} async-done(((f32[16,48,72]{2,1,0:T(8,128)}), f32[16,48,72]{2,1,0:T(8,128)S(1)}, u32[]{:S(2)}, u32[]{:S(2)}) %all-to-all-start.5) | async-done | bytes 221216 | tf_op jit(solution)/shard_map/all_to_all | solution.py:123
  191.7 12.4 %all-to-all-start.4 = ((bf16[16,256,72]{1,2,0:T(8,128)(2,1)}), bf16[16,256,72]{1,2,0:T(8,128)(2,1)S(1)}, u32[]{:S(2)}, u32[]{:S(2)}) async-start(bf16[16,256,72]{1,2,0:T(8,128)(2,1)} %copy.69), calls=%async_computation.4 | async-start | bytes 1179648 | tf_op jit(solution)/shard_map/all_to_all | solution.py:121
  204.2 2.3 copy.66
  206.5 2.3 all_to_all.83
  208.8 2.1 copy.67
  210.9 18.2 %all-to-all-done.4 = bf16[16,256,72]{1,2,0:T(8,128)(2,1)S(1)} async-done(((bf16[16,256,72]{1,2,0:T(8,128)(2,1)}), bf16[16,256,72]{1,2,0:T(8,128)(2,1)S(1)}, u32[]{:S(2)}, u32[]{:S(2)}) %all-to-all-start.4) | async-done | bytes 589856 | tf_op jit(solution)/shard_map/all_to_all | solution.py:121
  229.1 12.2 %all-to-all-start.3 = ((bf16[16,256,72]{1,2,0:T(8,128)(2,1)}), bf16[16,256,72]{1,2,0:T(8,128)(2,1)}, u32[]{:S(2)}, u32[]{:S(2)}) async-start(bf16[16,256,72]{1,2,0:T(8,128)(2,1)} %copy.67), calls=%async_computation.3 | async-start | bytes 1179648 | tf_op jit(solution)/shard_map/all_to_all | solution.py:120
  241.4 1.6 fusion.40
  246.0 132.5 %all-reduce.4.cloned.1.call-done = bf16[1152,72]{0,1:T(8,128)(2,1)} async-done(((bf16[1152,72]{0,1:T(8,128)(2,1)}), bf16[1152,72]{0,1:T(8,128)(2,1)}) %all-reduce.4.cloned.1.call-update) | async-done | bytes 165904
  380.1 1.5 convert_bitcast_fusion
  382.7 2.1 copy.72
  (77 shorter events, 25.3 us)
Async XLA Ops:
  8.0 77.8 %copy-start = (bf16[1,768,1152]{2,1,0:T(8,128)(2,1)S(1)}, bf16[1,768,1152]{2,1,0:T(8,128)(2,1)}, u32[]{:S(2)}) copy-start(bf16[1,768,1152]{2,1,0:T(8,128)(2,1)} %param.12) | copy-start | bytes 5308420
  8.0 77.8 %copy-start.2 = (bf16[72,1152]{1,0:T(8,128)(2,1)S(1)}, bf16[72,1152]{1,0:T(8,128)(2,1)}, u32[]{:S(2)}) copy-start(bf16[72,1152]{1,0:T(8,128)(2,1)} %param.13) | copy-start | bytes 497668
  10.1 37.3 %copy-start.1 = (bf16[1,256,1152]{2,1,0:T(8,128)(2,1)S(1)}, bf16[1,256,1152]{2,1,0:T(8,128)(2,1)}, u32[]{:S(2)}) copy-start(bf16[1,256,1152]{2,1,0:T(8,128)(2,1)} %param.11) | copy-start | bytes 1769476
  10.1 28.4 %all-to-all-start.1 = ((bf16[48,16,72]{2,0,1:T(8,128)(2,1)}), bf16[48,16,72]{2,0,1:T(8,128)(2,1)S(1)}, u32[]{:S(2)}, u32[]{:S(2)}) async-start(bf16[48,16,72]{2,0,1:T(8,128)(2,1)} %copy.57), calls=%async_computation.1 | async-start | bytes 393216 | tf_op jit(solution)/shard_map/all_to_all | solution.py:107
  38.6 34.1 %all-to-all-start = ((bf16[256,16,72]{0,2,1:T(8,128)(2,1)}), bf16[256,16,72]{0,2,1:T(8,128)(2,1)S(1)}, u32[]{:S(2)}, u32[]{:S(2)}) async-start(bf16[256,16,72]{0,2,1:T(8,128)(2,1)} %bitcast), calls=%async_computation | async-start | bytes 1179648 | tf_op jit(solution)/shard_map/all_to_all | solution.py:108
  72.7 38.4 %all-to-all-start.2 = ((bf16[256,16,72]{0,2,1:T(8,128)(2,1)}), bf16[256,16,72]{0,2,1:T(8,128)(2,1)}, u32[]{:S(2)}, u32[]{:S(2)}) async-start(bf16[256,16,72]{0,2,1:T(8,128)(2,1)} %bitcast.5), calls=%async_computation.2 | async-start | bytes 1179648 | tf_op jit(solution)/shard_map/all_to_all | solution.py:109
  163.9 27.8 %all-to-all-start.5 = ((f32[16,48,72]{2,1,0:T(8,128)}), f32[16,48,72]{2,1,0:T(8,128)S(1)}, u32[]{:S(2)}, u32[]{:S(2)}) async-start(f32[16,48,72]{2,1,0:T(8,128)} %bitcast.22), calls=%async_computation.5 | async-start | bytes 786432 | tf_op jit(solution)/shard_map/all_to_all | solution.py:123
  191.7 37.3 %all-to-all-start.4 = ((bf16[16,256,72]{1,2,0:T(8,128)(2,1)}), bf16[16,256,72]{1,2,0:T(8,128)(2,1)S(1)}, u32[]{:S(2)}, u32[]{:S(2)}) async-start(bf16[16,256,72]{1,2,0:T(8,128)(2,1)} %copy.69), calls=%async_computation.4 | async-start | bytes 1179648 | tf_op jit(solution)/shard_map/all_to_all | solution.py:121
  229.1 153.6 %all-to-all-start.3 = ((bf16[16,256,72]{1,2,0:T(8,128)(2,1)}), bf16[16,256,72]{1,2,0:T(8,128)(2,1)}, u32[]{:S(2)}, u32[]{:S(2)}) async-start(bf16[16,256,72]{1,2,0:T(8,128)(2,1)} %copy.67), calls=%async_computation.3 | async-start | bytes 1179648 | tf_op jit(solution)/shard_map/all_to_all | solution.py:120
  241.3 137.2 %all-reduce.4.cloned.1.call-start = ((), (), s32[]{:S(2)}) async-start(), calls=%async_computation.7 | async-start | bytes 331776
  243.0 137.1 %reduce-scatter.6.cloned.1.call-start = ((), (), s32[]{:S(2)}) async-start(), calls=%async_computation.8 | async-start | bytes 331776
Sparse Core Ops, SparseCore 0:
  245.4 133.0 all-reduce.3
Sparse Core Ops, SparseCore 1:
  246.8 23.9 reduce-scatter.5
where the time goes:
time: 394 us; the launch traced here: 392 us
  waiting for transfers between devices  216 us (55%)
  starting transfers between devices  75.6 us (19%)
  matrix products  38.2 us (10%)
  local copies, waits for them, and re-layouts  31.1 us (8%)
  between operations  16.3 us (4%)
  blocking collectives  9.54 us (2%)
  other arithmetic  5.01 us (1%)
    unnamed x4, waiting for transfers between devices  133 us
    all_to_all x1, waiting for transfers between devices, on_device(): lax.all_to_all(key_rows, 'seq', split_axis=1, concat_axis=0, tiled=True)  24.2 us
    all_to_all x1, waiting for transfers between devices, on_device(): lax.all_to_all(value_rows, 'seq', split_axis=1, concat_axis=0, tiled=True)  20.7 us
    all_to_all x1, waiting for transfers between devices, on_device(): lax.all_to_all(value_grad, 'seq', split_axis=0, concat_axis=1, tiled=True)  18.2 us
    all_to_all x1, starting transfers between devices, on_device(): lax.all_to_all(query_rows, 'seq', split_axis=1, concat_axis=0, tiled=True)  15.9 us
    all_to_all x1, starting transfers between devices, on_device(): lax.all_to_all(query_grad, 'seq', split_axis=0, concat_axis=1, tiled=True)  13.1 us
    all_to_all x1, starting transfers between devices, on_device(): lax.all_to_all(value_rows, 'seq', split_axis=1, concat_axis=0, tiled=True)  13.1 us
    dot_general x8, matrix products, scores_of(): jnp.einsum('rhd,nhd->hrn', query_heads, key_part, preferred_element_type=...  12.8 us
  transfers between devices with their start and end apart: 8, of which 6 were waited for; matrix products, arithmetic and copies ran while one was open for 6% of the time, Pallas kernels for 0%

commit v1 on v0

v1 whole, which is shorter than its diff:
```python
import math

import jax
import jax.numpy as jnp
from jax import lax
from jax.experimental import pallas as pl
from jax.experimental.pallas import tpu as pltpu
from jax.sharding import Mesh
from jax.sharding import PartitionSpec as P

HD = 72
ROWS = 768
FACTOR = 1.0 / math.sqrt(HD)
SCALE = FACTOR * math.log2(math.e)
BF = jnp.bfloat16
F32 = jnp.float32
CUBE = ("j", "kv")
DP = ("y", "xh", "core")
SEQ = ("t", "j")
PARAMS = pltpu.CompilerParams(vmem_limit_bytes=48 * 1024 * 1024)
PARAMS_SEQ = pltpu.CompilerParams(
    vmem_limit_bytes=48 * 1024 * 1024, dimension_semantics=("arbitrary",)
)


def heads_of(place):
    j, v = place // 2, place % 2
    return (8 * v + j, 8 * v + 4 + j)


def nn(a, b):
    return lax.dot_general(a, b, (((1,), (0,)), ((), ())), preferred_element_type=F32)


def pack_keys_kernel(k_ref, q_ref, o_ref):
    turned = k_ref[...].astype(F32).T
    rows = q_ref[...].astype(F32)
    for place in range(8):
        a, b = heads_of(place)
        o_ref[place, 0:144, :] = jnp.concatenate(
            [turned[HD * a : HD * a + HD], turned[HD * b : HD * b + HD]], axis=0
        ).astype(BF)
        qa = rows[:, HD * a : HD * a + HD]
        qb = rows[:, HD * b : HD * b + HD]
        middle = jnp.concatenate([qa[16:24], qb[0:8]], axis=0)
        o_ref[place, 144:160, :] = jnp.concatenate(
            [qa[0:16], middle, qb[8:24], jnp.zeros((16, 40), F32)], axis=1
        ).astype(BF)


def pack_values_kernel(v_ref, o_ref):
    turned = v_ref[...].astype(F32).T
    for place in range(8):
        a, b = heads_of(place)
        o_ref[place] = jnp.concatenate(
            [turned[HD * a : HD * a + HD], turned[HD * b : HD * b + HD]], axis=0
        ).astype(BF)


def unpack_kernel(g_ref, k_ref, v_ref):
    for part, o_ref in ((0, k_ref), (1, v_ref)):
        heads = [None] * 16
        for place in range(8):
            block = g_ref[place, 144 * part : 144 * part + 144, :].astype(F32)
            a, b = heads_of(place)
            heads[a] = block[0:HD]
            heads[b] = block[HD : 2 * HD]
        o_ref[...] = jnp.concatenate(heads, axis=0).T.astype(BF)


def first_kernel(kq_ref, v_ref, qg_ref, ga_ref, st_ref, ot_ref, q_ref, qs_ref, qt_ref):
    step = pl.program_id(0)

    @pl.when(step == 0)
    def _():
        for block in range(32):
            piece = qg_ref[block].astype(F32)
            base = 24 * block
            qs_ref[0, base : base + 16, :] = piece[:, 0:72]
            qs_ref[0, base + 16 : base + 24, :] = piece[0:8, 72:144]
            qs_ref[1, base : base + 8, :] = piece[8:16, 72:144]
            qs_ref[1, base + 8 : base + 24, :] = piece[:, 144:216]
        for h in range(2):
            q_ref[h] = qs_ref[h].astype(BF)
            qt_ref[h] = qs_ref[h].T.astype(BF)
        st_ref[0:2, :] = jnp.full((2, ROWS), -1e30, F32)
        st_ref[2:8, :] = jnp.zeros((6, ROWS), F32)
        ot_ref[...] = jnp.zeros_like(ot_ref)

    keys = kq_ref[0, 0:144, :].astype(F32)
    values = v_ref[0].astype(F32)
    for h in range(2):
        kh = keys[HD * h : HD * h + HD].T.astype(BF)
        vt = values[HD * h : HD * h + HD]
        vh = vt.T.astype(BF)
        s = nn(kh, qt_ref[h])
        u = nn(vh, ga_ref[h])
        before = st_ref[h : h + 1, :]
        highest = jnp.maximum(before, jnp.max(s, axis=0, keepdims=True))
        again = jnp.exp2((before - highest) * SCALE)
        e = jnp.exp2((s - highest) * SCALE)
        st_ref[h : h + 1, :] = highest
        st_ref[2 + h : 3 + h, :] = st_ref[2 + h : 3 + h, :] * again + jnp.sum(
            e, axis=0, keepdims=True
        )
        st_ref[4 + h : 5 + h, :] = st_ref[4 + h : 5 + h, :] * again + jnp.sum(
            e * u, axis=0, keepdims=True
        )
        ot_ref[h] = ot_ref[h] * again + nn(vt.astype(BF), e.astype(BF))


def joined(sg_ref, h):
    tops = [sg_ref[t, h : h + 1, :] for t in range(4)]
    highest = jnp.maximum(jnp.maximum(tops[0], tops[1]), jnp.maximum(tops[2], tops[3]))
    total = jnp.zeros((1, ROWS), F32)
    weighted = jnp.zeros((1, ROWS), F32)
    for t in range(4):
        part = jnp.exp2((tops[t] - highest) * SCALE)
        total = total + sg_ref[t, 2 + h : 3 + h, :] * part
        weighted = weighted + sg_ref[t, 4 + h : 5 + h, :] * part
    return highest, total, weighted / total


def weight_kernel(sg_ref, st_ref, ot_ref, go_ref, o_ref):
    rows = []
    for h in range(2):
        highest, total, _ = joined(sg_ref, h)
        share = jnp.exp2((st_ref[h : h + 1, :] - highest) * SCALE) / total
        rows.append(ot_ref[h] * share)
    attn = jnp.concatenate(rows, axis=0).astype(BF)
    o_ref[...] = nn(attn, go_ref[...]).T.astype(BF)


def second_kernel(
    kq_ref, v_ref, q_ref, ga_ref, sg_ref, kv_ref, dq_ref, qt_ref, gn_ref, stat_ref, dqt_ref
):
    step = pl.program_id(0)

    @pl.when(step == 0)
    def _():
        for h in range(2):
            qt_ref[h] = q_ref[h].astype(F32).T.astype(BF)
            gn_ref[h] = ga_ref[h].astype(F32).T.astype(BF)
            highest, total, delta = joined(sg_ref, h)
            stat_ref[h : h + 1, :] = highest
            stat_ref[2 + h : 3 + h, :] = 1.0 / total
            stat_ref[4 + h : 5 + h, :] = delta
        dqt_ref[...] = jnp.zeros_like(dqt_ref)

    keys = kq_ref[0, 0:144, :].astype(F32)
    values = v_ref[0].astype(F32)
    for h in range(2):
        kt = keys[HD * h : HD * h + HD]
        kh = kt.T.astype(BF)
        vh = values[HD * h : HD * h + HD].T.astype(BF)
        s = nn(kh, qt_ref[h])
        u = nn(vh, ga_ref[h])
        p = jnp.exp2((s - stat_ref[h : h + 1, :]) * SCALE) * stat_ref[2 + h : 3 + h, :]
        ds = (p * (u - stat_ref[4 + h : 5 + h, :])).astype(BF)
        dv = nn(p.astype(BF), gn_ref[h])
        dk = nn(ds, q_ref[h]) * FACTOR
        dqt_ref[HD * h : HD * h + HD, :] += nn(kt.astype(BF), ds)
        if h == 0:
            dk0, dv0 = dk, dv
    kv_ref[0, 0:144, :] = jnp.concatenate([dk0.T, dk.T], axis=0).astype(BF)
    kv_ref[0, 144:288, :] = jnp.concatenate([dv0.T, dv.T], axis=0).astype(BF)

    @pl.when(step == pl.num_programs(0) - 1)
    def _():
        dq_ref[...] = (dqt_ref[...] * FACTOR).T.astype(BF)


def whole(*shape):
    return pl.BlockSpec(shape, lambda i: (0,) * len(shape))


def block(*shape):
    return pl.BlockSpec((1,) + shape, lambda i: (i,) + (0,) * len(shape))


def on_device(slab_queries, key_tokens, value_tokens, grad_output, out_weight):
    query_rows = slab_queries[0]
    key_rows = key_tokens[0]
    value_rows = value_tokens[0]
    cotangent = grad_output[0]
    t = lax.axis_index("t")
    v = lax.axis_index("kv")
    swap = [(0, 1), (1, 0)]

    query_half = lax.dynamic_slice_in_dim(query_rows, 24 * v, 24, 0)
    packed_keys = pl.pallas_call(
        pack_keys_kernel,
        out_shape=jax.ShapeDtypeStruct((8, 160, 256), BF),
        compiler_params=PARAMS,
        name="pack_keys",
    )(key_rows, query_half)
    keys = lax.all_to_all(packed_keys, CUBE, 0, 0, tiled=True)

    cotangent_half = lax.dynamic_slice_in_dim(cotangent, 384 * v, 384, 0)
    grad_half = lax.dot_general(
        out_weight, cotangent_half, (((1,), (1,)), ((), ())), preferred_element_type=F32
    ).astype(BF)
    grad_four = lax.all_gather(grad_half, "t")
    grad_keep = lax.dynamic_slice_in_dim(grad_four, 2 * v, 2, 0)
    grad_sent = lax.dynamic_slice_in_dim(grad_four, 2 - 2 * v, 2, 0)
    grad_come = lax.ppermute(grad_sent, "kv", swap)
    grad_heads = jnp.where(
        v == 0,
        jnp.concatenate([grad_keep, grad_come], axis=2),
        jnp.concatenate([grad_come, grad_keep], axis=2),
    )

    packed_values = pl.pallas_call(
        pack_values_kernel,
        out_shape=jax.ShapeDtypeStruct((8, 144, 256), BF),
        compiler_params=PARAMS,
        name="pack_values",
    )(value_rows)
    values = lax.all_to_all(packed_values, CUBE, 0, 0, tiled=True)

    query_pieces = lax.all_gather(keys[:, 144:160, :].reshape(128, 256), "t")
    query_pieces = query_pieces.reshape(32, 16, 256)

    stats, attn_turned, queries = pl.pallas_call(
        first_kernel,
        grid=(8,),
        in_specs=[block(160, 256), block(144, 256), whole(32, 16, 256), whole(2, HD, ROWS)],
        out_specs=[whole(8, ROWS), whole(2, HD, ROWS), whole(2, ROWS, HD)],
        out_shape=[
            jax.ShapeDtypeStruct((8, ROWS), F32),
            jax.ShapeDtypeStruct((2, HD, ROWS), F32),
            jax.ShapeDtypeStruct((2, ROWS, HD), BF),
        ],
        scratch_shapes=[pltpu.VMEM((2, ROWS, HD), F32), pltpu.VMEM((2, HD, ROWS), BF)],
        compiler_params=PARAMS_SEQ,
        name="first_pass",
    )(keys, values, query_pieces, grad_heads)

    gathered = lax.all_gather(stats, "t")

    weight_turned = pl.pallas_call(
        weight_kernel,
        out_shape=jax.ShapeDtypeStruct((1152, 144), BF),
        compiler_params=PARAMS,
        name="weight_part",
    )(gathered, stats, attn_turned, cotangent)
    weight_come = lax.all_to_all(weight_turned, DP, 0, 0, tiled=True)

    grads, query_grad = pl.pallas_call(
        second_kernel,
        grid=(8,),
        in_specs=[
            block(160, 256),
            block(144, 256),
            whole(2, ROWS, HD),
            whole(2, HD, ROWS),
            whole(4, 8, ROWS),
        ],
        out_specs=[block(288, 256), whole(ROWS, 144)],
        out_shape=[
            jax.ShapeDtypeStruct((8, 288, 256), BF),
            jax.ShapeDtypeStruct((ROWS, 144), BF),
        ],
        scratch_shapes=[
            pltpu.VMEM((2, HD, ROWS), BF),
            pltpu.VMEM((2, ROWS, HD), BF),
            pltpu.VMEM((8, ROWS), F32),
            pltpu.VMEM((144, ROWS), F32),
        ],
        compiler_params=PARAMS_SEQ,
        name="second_pass",
    )(keys, values, queries, grad_heads, gathered)

    query_sum = lax.psum_scatter(query_grad, "t", scatter_dimension=0, tiled=True)
    grads_back = lax.all_to_all(grads, CUBE, 0, 0, tiled=True)
    key_out, value_out = pl.pallas_call(
        unpack_kernel,
        out_shape=[jax.ShapeDtypeStruct((256, 1152), BF)] * 2,
        compiler_params=PARAMS,
        name="unpack_grads",
    )(grads_back)

    query_back = lax.all_to_all(query_sum, CUBE, 0, 0, tiled=True)
    query_out = (
        query_back.reshape(4, 2, 24, 2, HD).transpose(2, 1, 3, 0, 4).reshape(24, 1152)
    )

    weight_sum = jnp.sum(weight_come.astype(F32).reshape(16, HD, 144), axis=0)
    weight_all = jnp.sum(lax.all_gather(weight_sum, "t"), axis=0)
    weight_head = jnp.where(t % 2 == 0, weight_all[:, 0:HD], weight_all[:, HD : 2 * HD])
    weight_low, weight_high = weight_head[0:36], weight_head[36:72]
    weight_sent = jnp.where(v == 0, weight_high, weight_low)
    weight_keep = jnp.where(v == 0, weight_low, weight_high)
    weight_other = lax.ppermute(weight_sent, "kv", swap)
    weight_out = jnp.where(v == t // 2, weight_keep, weight_other).T
    return (key_out[None], value_out[None], query_out[None], weight_out)


def solution(mesh):
    cube = Mesh(mesh.devices.reshape(4, 2, 2, 4, 4, 2), DP + SEQ + ("kv",))
    return jax.shard_map(
        on_device,
        mesh=cube,
        in_specs=(
            P(DP, SEQ, None),
            P(DP, SEQ + ("kv",), None),
            P(DP, SEQ + ("kv",), None),
            P(DP, None, None),
            P(SEQ, None),
        ),
        out_specs=(
            P(DP, SEQ + ("kv",), None),
            P(DP, SEQ + ("kv",), None),
            P(DP, SEQ + ("kv",), None),
            P(SEQ, DP + ("kv",)),
        ),
        check_vma=False,
    )
```

time: 394 us -> 255 us (0.65)
  the two profiles are of different devices: /device:TPU:1 before, /device:TPU:64 now
where the time goes in v1:
time: 255 us; the launch traced here: 254 us
  blocking collectives  146 us (57%)
  waiting for transfers between devices  33.2 us (13%)
  starting transfers between devices  26.4 us (10%)
  Pallas kernels  25.1 us (10%)
  between operations  14.2 us (6%)
  local copies, waits for them, and re-layouts  7.82 us (3%)
    all_gather x1, blocking collectives, on_device(): weight_all = jnp.sum(lax.all_gather(weight_sum, 't'), axis=0)  44.2 us
    all_gather x1, blocking collectives, on_device(): grad_four = lax.all_gather(grad_half, 't')  33.8 us
    all_to_all x1, blocking collectives, on_device(): weight_come = lax.all_to_all(weight_turned, DP, 0, 0, tiled=True)  19.8 us
    all_gather x1, blocking collectives, on_device(): query_pieces = lax.all_gather(keys[:, 144:160, :].reshape(128, 256), 't')  18.7 us
    all_gather x1, blocking collectives, on_device(): gathered = lax.all_gather(stats, 't')  17.3 us
    reduce_scatter x1, waiting for transfers between devices, on_device(): lax.psum_scatter(query_grad, 't', scatter_dimension=0, tiled=True)  14.8 us
    all_to_all x1, waiting for transfers between devices, on_device(): keys = lax.all_to_all(packed_keys, CUBE, 0, 0, tiled=True)  11.9 us
    all_to_all x1, blocking collectives, on_device(): query_back = lax.all_to_all(query_sum, CUBE, 0, 0, tiled=True)  11.6 us
  transfers between devices with their start and end apart: 6, of which 4 were waited for; matrix products, arithmetic and copies ran while one was open for 1% of the time, Pallas kernels for 0%

profile of v1, /device:TPU:64, one launch (start us, length us, event | category | flops | bytes accessed | tf_op | source)
XLA Modules:
  0.0 254.5 jit_solution(3469857575738945991)
XLA Ops:
  7.2 0.0 copy-start
  7.2 0.9 dynamic-slice_bitcast_fusion.q_ref
  8.0 1.1 copy-done.4
  9.1 1.2 pack_keys.1
  10.3 8.6 %all-to-all-start = ((bf16[8,160,256]{2,1,0:T(8,128)(2,1)}), bf16[8,160,256]{2,1,0:T(8,128)(2,1)S(1)}, u32[]{:S(2)}, u32[]{:S(2)}) async-start(bf16[8,160,256]{2,1,0:T(8,128)(2,1)} %pack_keys.1), calls=%async_computation | async-start | bytes 1310720 | tf_op jit(solution)/shard_map/all_to_all | solution.py:197
  18.9 0.0 copy-done.5
  18.9 0.2 pack_values.1
  19.2 0.0 copy-start.2
  19.2 0.8 copy-done.2
  20.0 11.9 %all-to-all-done.kq_ref = bf16[8,160,256]{2,1,0:T(8,128)(2,1)S(1)} async-done(((bf16[8,160,256]{2,1,0:T(8,128)(2,1)}), bf16[8,160,256]{2,1,0:T(8,128)(2,1)S(1)}, u32[]{:S(2)}, u32[]{:S(2)}) %all-to-all-start) | async-done | bytes 655392 | tf_op jit(solution)/shard_map/all_to_all | solution.py:197
  31.9 6.0 %all-to-all-start.1 = ((bf16[8,144,256]{2,1,0:T(8,128)(2,1)}), bf16[8,144,256]{2,1,0:T(8,128)(2,1)S(1)}, u32[]{:S(2)}, u32[]{:S(2)}) async-start(bf16[8,144,256]{2,1,0:T(8,128)(2,1)} %copy-done.2), calls=%async_computation.1 | async-start | bytes 1179648 | tf_op jit(solution)/shard_map/all_to_all | solution.py:219
  37.9 0.0 reduce-scatter.2.cloned.1.call-start
  37.9 0.0 copy-done
  37.9 0.0 copy-done.1
  37.9 0.4 fusion
  38.4 33.8 %all-gather = bf16[288,384]{1,0:T(8,128)(2,1)S(1)} all-gather(bf16[72,384]{1,0:T(8,128)(2,1)S(1)} %fusion), channel_id=2, replica_groups=mesh['y'=4,'xh'=2,'core'=2,'t'=4,'j'=4,'kv'=2] {'t'}, dimensions={0}, use_global_device_ids=true | all-gather | bytes 276480 | tf_op jit(solution)/shard_map/all_gather | solution.py:203
  72.2 3.0 %collective-permute-start = (bf16[2,72,384]{2,1,0:T(8,128)(2,1)S(1)}, bf16[2,72,384]{2,1,0:T(8,128)(2,1)S(1)}, u32[]{:S(2)}, u32[]{:S(2)}) collective-permute-start(bf16[2,72,384]{2,1,0:T(8,128)(2,1)S(1)} %get-tuple-element.19), channel_id=1, source_target_pairs={{0,1},{1,0},{2,3},{3,2},{4,5},{5,4},{6,7},{7,6},{8,9},{9,8},{10,11... | collective-permute-start | bytes 331784 | tf_op jit(solution)/shard_map/ppermute | solution.py:206
  75.2 3.6 %collective-permute-done = bf16[2,72,384]{2,1,0:T(8,128)(2,1)S(1)} collective-permute-done((bf16[2,72,384]{2,1,0:T(8,128)(2,1)S(1)}, bf16[2,72,384]{2,1,0:T(8,128)(2,1)S(1)}, u32[]{:S(2)}, u32[]{:S(2)}) %collective-permute-start) | collective-permute-done | bytes 110624 | tf_op jit(solution)/shard_map/ppermute | solution.py:206
  78.8 0.6 copy-done.9
  79.5 1.0 maximum_select_fusion.ga_ref
  80.5 18.7 %all_gather.21 = bf16[4,128,256]{2,1,0:T(8,128)(2,1)} all-gather(bf16[1,128,256]{2,1,0:T(8,128)(2,1)S(1)} %bitcast.35), channel_id=1, replica_groups=mesh['y'=4,'xh'=2,'core'=2,'t'=4,'j'=4,'kv'=2] {'t'}, dimensions={0}, use_global_device_ids=true | all-gather | bytes 327680 | tf_op jit(solution)/shard_map/all_gather | solution.py:221
  99.2 0.0 all-to-all-done.1.v_ref
  99.2 1.0 copy-done.3
  100.2 10.6 %first_pass.1 = (f32[8,768]{1,0:T(8,128)S(1)}, f32[2,72,768]{2,1,0:T(8,128)S(1)}, bf16[2,768,72]{2,1,0:T(8,128)(2,1)S(1)}) custom-call(bf16[8,160,256]{2,1,0:T(8,128)(2,1)S(1)} %all-to-all-done.kq_ref, bf16[8,144,256]{2,1,0:T(8,128)(2,1)S(1)} %all-to-all-done.1.v_ref, bf16[32,16,256]{2,1,0:T(8,128)(2,1)S(1)} %bitcast.27, ...), custom_call_target="tpu_custom_call" | custom-call | tf_op jit(solution)/shard_map/first_pass/pallas_call | solution.py:224
  110.8 0.0 copy-start.6
  110.8 0.8 copy-done.6
  111.6 17.3 %all-gather.1 = f32[32,768]{1,0:T(8,128)S(1)} all-gather(f32[8,768]{1,0:T(8,128)S(1)} %get-tuple-element.12.st_ref), channel_id=3, replica_groups=mesh['y'=4,'xh'=2,'core'=2,'t'=4,'j'=4,'kv'=2] {'t'}, dimensions={0}, use_global_device_ids=true | all-gather | bytes 122880 | tf_op jit(solution)/shard_map/all_gather | solution.py:239
  128.9 11.1 %second_pass.1 = (bf16[8,288,256]{2,1,0:T(8,128)(2,1)}, bf16[768,144]{1,0:T(8,128)(2,1)S(1)}) custom-call(bf16[8,160,256]{2,1,0:T(8,128)(2,1)S(1)} %all-to-all-done.kq_ref, bf16[8,144,256]{2,1,0:T(8,128)(2,1)S(1)} %all-to-all-done.1.v_ref, bf16[2,768,72]{2,1,0:T(8,128)(2,1)S(1)} %get-tuple-element.11.q_ref, ...), custom_call_target="tpu_custom_call" | custom-call | tf_op jit(solution)/shard_map/second_pass/pallas_call | solution.py:249
  140.1 0.7 copy-done.8
  140.8 0.0 reduce-scatter.2.cloned.1.call-update
  140.8 0.0 copy-start.7
  140.8 1.0 copy-done.7
  141.8 0.6 weight_part.1
  142.4 19.8 %all_to_all.33 = bf16[16,72,144]{2,1,0:T(8,128)(2,1)S(1)} all-to-all(bf16[16,72,144]{2,1,0:T(8,128)(2,1)S(1)} %bitcast.26), channel_id=1, replica_groups=mesh['y'=4,'xh'=2,'core'=2,'t'=4,'j'=4,'kv'=2] {'y','xh','core'}, dimensions={0} | all-to-all | bytes 663552 | tf_op jit(solution)/shard_map/all_to_all | solution.py:247
  162.2 14.8 %reduce-scatter.2.cloned.1.call-done = bf16[192,144]{1,0:T(8,128)(2,1)} async-done(((bf16[768,144]{1,0:T(8,128)(2,1)}), bf16[192,144]{1,0:T(8,128)(2,1)}) %reduce-scatter.2.cloned.1.call-update) | async-done | bytes 55312 | tf_op jit(solution)/shard_map/reduce_scatter | solution.py:274
  177.0 11.6 %all_to_all.34 = bf16[8,24,144]{2,1,0:T(8,128)(2,1)S(1)} all-to-all(bf16[8,24,144]{2,1,0:T(8,128)(2,1)} %bitcast.36), channel_id=1, replica_groups=mesh['y'=4,'xh'=2,'core'=2,'t'=4,'j'=4,'kv'=2] {'j','kv'}, dimensions={0} | all-to-all | bytes 110592 | tf_op jit(solution)/shard_map/all_to_all | solution.py:283
  188.7 6.0 %all-to-all-start.2 = ((bf16[8,288,256]{2,1,0:T(8,128)(2,1)}), bf16[8,288,256]{2,1,0:T(8,128)(2,1)S(1)}, u32[]{:S(2)}, u32[]{:S(2)}) async-start(bf16[8,288,256]{2,1,0:T(8,128)(2,1)} %get-tuple-element.13), calls=%async_computation.2 | async-start | bytes 2359296 | tf_op jit(solution)/shard_map/all_to_all | solution.py:275
  194.6 0.1 convert_reduce_fusion
  194.8 44.2 %all-gather.2 = f32[288,144]{1,0:T(8,128)S(1)} all-gather(f32[72,144]{1,0:T(8,128)S(1)} %convert_reduce_fusion), channel_id=4, replica_groups=mesh['y'=4,'xh'=2,'core'=2,'t'=4,'j'=4,'kv'=2] {'t'}, dimensions={0}, use_global_device_ids=true | all-gather | bytes 207360 | tf_op jit(solution)/shard_map/all_gather | solution.py:289
  239.0 0.1 slice_select_fusion
  239.1 2.8 %collective-permute-start.1 = (f32[36,72]{1,0:T(8,128)S(1)}, f32[36,72]{1,0:T(8,128)S(1)}, u32[]{:S(2)}, u32[]{:S(2)}) collective-permute-start(f32[36,72]{1,0:T(8,128)S(1)} %slice_select_fusion.1), channel_id=1, source_target_pairs={{0,1},{1,0},{2,3},{3,2},{4,5},{5,4},{6,7},{7,6},{8,9},{9,8},{10,11... | collective-permute-start | bytes 31112 | tf_op jit(solution)/shard_map/ppermute | solution.py:294
  241.9 2.9 %collective-permute-done.1 = f32[36,72]{1,0:T(8,128)S(1)} collective-permute-done((f32[36,72]{1,0:T(8,128)S(1)}, f32[36,72]{1,0:T(8,128)S(1)}, u32[]{:S(2)}, u32[]{:S(2)}) %collective-permute-start.1) | collective-permute-done | bytes 10400 | tf_op jit(solution)/shard_map/ppermute | solution.py:294
  244.8 0.6 select_bitcast_fusion
  245.4 0.1 reshape.23
  245.5 0.1 copy.13
  245.6 0.8 broadcast_in_dim_reshape.3
  246.3 0.0 all-to-all-done.2.g_ref
  246.3 1.3 unpack_grads.1
  (10 shorter events, 0.1 us)
Async XLA Ops:
  7.2 30.7 %copy-start = (bf16[72,1152]{1,0:T(8,128)(2,1)S(1)}, bf16[72,1152]{1,0:T(8,128)(2,1)}, u32[]{:S(2)}) copy-start(bf16[72,1152]{1,0:T(8,128)(2,1)} %param.9) | copy-start | bytes 497668
  8.0 1.1 copy-start.4
  9.1 9.8 %copy-start.5 = (bf16[1,256,1152]{2,1,0:T(8,128)(2,1)S(1)}, bf16[1,256,1152]{2,1,0:T(8,128)(2,1)}, u32[]{:S(2)}) copy-start(bf16[1,256,1152]{2,1,0:T(8,128)(2,1)} %param.7) | copy-start | bytes 1769476
  10.3 27.6 %copy-start.1 = (bf16[1,768,1152]{2,1,0:T(8,128)(2,1)S(1)}, bf16[1,768,1152]{2,1,0:T(8,128)(2,1)}, u32[]{:S(2)}) copy-start(bf16[1,768,1152]{2,1,0:T(8,128)(2,1)} %param.8) | copy-start | bytes 5308420
  10.3 21.6 %all-to-all-start = ((bf16[8,160,256]{2,1,0:T(8,128)(2,1)}), bf16[8,160,256]{2,1,0:T(8,128)(2,1)S(1)}, u32[]{:S(2)}, u32[]{:S(2)}) async-start(bf16[8,160,256]{2,1,0:T(8,128)(2,1)} %pack_keys.1), calls=%async_computation | async-start | bytes 1310720 | tf_op jit(solution)/shard_map/all_to_all | solution.py:197
  19.2 0.8 copy-start.2
  31.9 67.3 %all-to-all-start.1 = ((bf16[8,144,256]{2,1,0:T(8,128)(2,1)}), bf16[8,144,256]{2,1,0:T(8,128)(2,1)S(1)}, u32[]{:S(2)}, u32[]{:S(2)}) async-start(bf16[8,144,256]{2,1,0:T(8,128)(2,1)} %copy-done.2), calls=%async_computation.1 | async-start | bytes 1179648 | tf_op jit(solution)/shard_map/all_to_all | solution.py:219
  37.9 139.1 %reduce-scatter.2.cloned.1.call-start = ((), (), s32[]{:S(2)}) async-start(), calls=%async_computation.6 | async-start | bytes 491520 | tf_op jit(solution)/shard_map/reduce_scatter | solution.py:274
  72.2 6.6 %collective-permute-start = (bf16[2,72,384]{2,1,0:T(8,128)(2,1)S(1)}, bf16[2,72,384]{2,1,0:T(8,128)(2,1)S(1)}, u32[]{:S(2)}, u32[]{:S(2)}) collective-permute-start(bf16[2,72,384]{2,1,0:T(8,128)(2,1)S(1)} %get-tuple-element.19), channel_id=1, source_target_pairs={{0,1},{1,0},{2,3},{3,2},{4,5},{5,4},{6,7},{7,6},{8,9},{9,8},{10,11... | collective-permute-start | bytes 331784 | tf_op jit(solution)/shard_map/ppermute | solution.py:206
  78.8 0.6 copy-start.9
  99.2 1.0 copy-start.3
  110.8 0.8 copy-start.6
  140.0 0.7 copy-start.8
  140.8 1.0 copy-start.7
  188.7 57.7 %all-to-all-start.2 = ((bf16[8,288,256]{2,1,0:T(8,128)(2,1)}), bf16[8,288,256]{2,1,0:T(8,128)(2,1)S(1)}, u32[]{:S(2)}, u32[]{:S(2)}) async-start(bf16[8,288,256]{2,1,0:T(8,128)(2,1)} %get-tuple-element.13), calls=%async_computation.2 | async-start | bytes 2359296 | tf_op jit(solution)/shard_map/all_to_all | solution.py:275
  239.1 5.7 %collective-permute-start.1 = (f32[36,72]{1,0:T(8,128)S(1)}, f32[36,72]{1,0:T(8,128)S(1)}, u32[]{:S(2)}, u32[]{:S(2)}) collective-permute-start(f32[36,72]{1,0:T(8,128)S(1)} %slice_select_fusion.1), channel_id=1, source_target_pairs={{0,1},{1,0},{2,3},{3,2},{4,5},{5,4},{6,7},{7,6},{8,9},{9,8},{10,11... | collective-permute-start | bytes 31112 | tf_op jit(solution)/shard_map/ppermute | solution.py:294
Sparse Core Ops, SparseCore 0:
  140.9 36.0 reduce-scatter.1

commit v2 on v1

v2 whole, which is shorter than its diff:
```python
import math

import jax
import jax.numpy as jnp
from jax import lax
from jax.experimental import pallas as pl
from jax.experimental.pallas import tpu as pltpu
from jax.sharding import Mesh
from jax.sharding import PartitionSpec as P

HD = 72
ROWS = 768
FACTOR = 1.0 / math.sqrt(HD)
SCALE = FACTOR * math.log2(math.e)
BF = jnp.bfloat16
F32 = jnp.float32
VMEM = 60 * 1024 * 1024
LONG = pl.CostEstimate(flops=60_000_000_000, bytes_accessed=200_000_000, transcendentals=0)
ANY = pl.BlockSpec(memory_space=pl.ANY)
SCALAR = pl.BlockSpec(memory_space=pltpu.SMEM)
HERE = pl.BlockSpec(memory_space=pltpu.VMEM)
CUBE = ("j", "kv")
DP = ("y", "xh", "core")
SEQ = ("t", "j")
PARAMS = pltpu.CompilerParams(vmem_limit_bytes=VMEM)
PARAMS_SEQ = pltpu.CompilerParams(
    vmem_limit_bytes=VMEM, dimension_semantics=("arbitrary",)
)


def heads_of(place):
    j, v = place // 2, place % 2
    return (8 * v + j, 8 * v + 4 + j)


def nn(a, b):
    return lax.dot_general(a, b, (((1,), (0,)), ((), ())), preferred_element_type=F32)


def pack_kernel(k_ref, v_ref, q_ref, o_ref):
    rows = q_ref[...].astype(F32)
    for first, ref in ((0, k_ref), (144, v_ref)):
        turned = ref[...].astype(F32).T
        for place in range(8):
            a, b = heads_of(place)
            o_ref[place, first : first + 144, :] = jnp.concatenate(
                [turned[HD * a : HD * a + HD], turned[HD * b : HD * b + HD]], axis=0
            ).astype(BF)
    for place in range(8):
        a, b = heads_of(place)
        qa = rows[:, HD * a : HD * a + HD]
        qb = rows[:, HD * b : HD * b + HD]
        middle = jnp.concatenate([qa[16:24], qb[0:8]], axis=0)
        o_ref[place, 288:304, :] = jnp.concatenate(
            [qa[0:16], middle, qb[8:24], jnp.zeros((16, 40), F32)], axis=1
        ).astype(BF)


def weight_sum_kernel(v_ref, w_ref, keep_ref, send_ref):
    total = jnp.zeros((48, 256), F32)
    for source in range(16):
        total = total + w_ref[source].astype(F32)
    rows = jnp.concatenate([total[:, 72 * k : 72 * k + 72] for k in range(3)], axis=0)
    low, high = rows[:, 0:36], rows[:, 36:72]
    keep_ref[...] = jnp.where(v_ref[0] == 0, low, high)
    send_ref[...] = jnp.where(v_ref[0] == 0, high, low)


def scatter_kernel(v_ref, g_ref, keep_ref, come_ref, o_ref):
    heads = [None] * 16
    for place in range(8):
        piece = g_ref[place].astype(F32)
        tail = jnp.concatenate(
            [
                piece[96 + 8 * (g // 8) : 104 + 8 * (g // 8), 16 * (g % 8) : 16 * (g % 8) + 16]
                for g in range(12)
            ],
            axis=0,
        )
        a, b = heads_of(place)
        heads[a] = piece[0:96, 0:72]
        heads[b] = jnp.concatenate([piece[0:96, 72:128], tail], axis=1)
    rows = jnp.concatenate(heads, axis=1)
    for t in range(4):
        i = t % 2
        mine = keep_ref[HD * i : HD * i + HD, :]
        other = come_ref[HD * i : HD * i + HD, :]
        weight = jnp.where(v_ref[0] == t // 2, mine, other)
        folded = [weight[8 * k : 8 * k + 8] for k in range(9)] + [jnp.zeros((8, 828), F32)]
        o_ref[t] = jnp.concatenate(
            [rows[24 * t : 24 * t + 24], jnp.concatenate(folded, axis=1)], axis=0
        ).astype(BF)


def finish_kernel(x_ref, q_ref, w_ref):
    q_ref[...] = x_ref[0:24, :]
    folded = x_ref[...].astype(F32)[24:32]
    for k in range(9):
        w_ref[8 * k : 8 * k + 8, :] = folded[:, 36 * k : 36 * k + 36]


def unpack_kernel(g_ref, after_ref, k_ref, v_ref):
    for part, o_ref in ((0, k_ref), (1, v_ref)):
        heads = [None] * 16
        for place in range(8):
            block = g_ref[place, 144 * part : 144 * part + 144, :].astype(F32)
            a, b = heads_of(place)
            heads[a] = block[0:HD]
            heads[b] = block[HD : 2 * HD]
        o_ref[...] = jnp.concatenate(heads, axis=0).T.astype(BF)


def first_kernel(
    place_ref, kv_ref, qg_ref, keep_ref, come_ref, st_ref, ot_ref, q_ref, ga_ref, qs_ref, qt_ref
):
    step = pl.program_id(0)

    @pl.when(step == 0)
    def _():
        for block in range(32):
            piece = qg_ref[block].astype(F32)
            base = 24 * block
            qs_ref[0, base : base + 16, :] = piece[:, 0:72]
            qs_ref[0, base + 16 : base + 24, :] = piece[0:8, 72:144]
            qs_ref[1, base : base + 8, :] = piece[8:16, 72:144]
            qs_ref[1, base + 8 : base + 24, :] = piece[:, 144:216]
        @pl.when(place_ref[0] == 0)
        def _():
            ga_ref[:, :, 0:384] = keep_ref[...]
            ga_ref[:, :, 384:768] = come_ref[...]

        @pl.when(place_ref[0] == 1)
        def _():
            ga_ref[:, :, 0:384] = come_ref[...]
            ga_ref[:, :, 384:768] = keep_ref[...]

        for h in range(2):
            q_ref[h] = qs_ref[h].astype(BF)
            qt_ref[h] = qs_ref[h].T.astype(BF)
        st_ref[0:2, :] = jnp.full((2, ROWS), -1e30, F32)
        st_ref[2:8, :] = jnp.zeros((6, ROWS), F32)
        ot_ref[...] = jnp.zeros_like(ot_ref)

    keys = kv_ref[0, 0:144, :].astype(F32)
    values = kv_ref[0, 144:288, :].astype(F32)
    for h in range(2):
        kh = keys[HD * h : HD * h + HD].T.astype(BF)
        vt = values[HD * h : HD * h + HD]
        vh = vt.T.astype(BF)
        s = nn(kh, qt_ref[h])
        u = nn(vh, ga_ref[h])
        before = st_ref[h : h + 1, :]
        highest = jnp.maximum(before, jnp.max(s, axis=0, keepdims=True))
        again = jnp.exp2((before - highest) * SCALE)
        e = jnp.exp2((s - highest) * SCALE)
        st_ref[h : h + 1, :] = highest
        st_ref[2 + h : 3 + h, :] = st_ref[2 + h : 3 + h, :] * again + jnp.sum(
            e, axis=0, keepdims=True
        )
        st_ref[4 + h : 5 + h, :] = st_ref[4 + h : 5 + h, :] * again + jnp.sum(
            e * u, axis=0, keepdims=True
        )
        ot_ref[h] = ot_ref[h] * again + nn(vt.astype(BF), e.astype(BF))


def joined(sg_ref, h):
    tops = [sg_ref[t, h : h + 1, :] for t in range(4)]
    highest = jnp.maximum(jnp.maximum(tops[0], tops[1]), jnp.maximum(tops[2], tops[3]))
    total = jnp.zeros((1, ROWS), F32)
    weighted = jnp.zeros((1, ROWS), F32)
    for t in range(4):
        part = jnp.exp2((tops[t] - highest) * SCALE)
        total = total + sg_ref[t, 2 + h : 3 + h, :] * part
        weighted = weighted + sg_ref[t, 4 + h : 5 + h, :] * part
    return highest, total, weighted / total


def weight_kernel(sg_ref, st_ref, ot_ref, go_ref, o_ref):
    rows = []
    for h in range(2):
        highest, total, _ = joined(sg_ref, h)
        share = jnp.exp2((st_ref[h : h + 1, :] - highest) * SCALE) / total
        rows.append(ot_ref[h] * share)
    attn = jnp.concatenate(rows, axis=0).astype(BF)
    product = nn(attn, go_ref[...])
    for c in range(16):
        part = product[:, HD * c : HD * c + HD]
        o_ref[c] = jnp.concatenate(
            [part[0:48], part[48:96], part[96:144], jnp.zeros((48, 40), F32)], axis=1
        ).astype(BF)


def second_kernel(
    kv_ref, q_ref, ga_ref, sg_ref, after_ref, grad_ref, dq_ref, qt_ref, gn_ref, stat_ref, dqt_ref
):
    step = pl.program_id(0)

    @pl.when(step == 0)
    def _():
        for h in range(2):
            qt_ref[h] = q_ref[h].astype(F32).T.astype(BF)
            gn_ref[h] = ga_ref[h].astype(F32).T.astype(BF)
            highest, total, delta = joined(sg_ref, h)
            stat_ref[h : h + 1, :] = highest
            stat_ref[2 + h : 3 + h, :] = 1.0 / total
            stat_ref[4 + h : 5 + h, :] = delta
        dqt_ref[...] = jnp.zeros_like(dqt_ref)

    keys = kv_ref[0, 0:144, :].astype(F32)
    values = kv_ref[0, 144:288, :].astype(F32)
    dks, dvs = [], []
    for h in range(2):
        kt = keys[HD * h : HD * h + HD]
        kh = kt.T.astype(BF)
        vh = values[HD * h : HD * h + HD].T.astype(BF)
        s = nn(kh, qt_ref[h])
        u = nn(vh, ga_ref[h])
        p = jnp.exp2((s - stat_ref[h : h + 1, :]) * SCALE) * stat_ref[2 + h : 3 + h, :]
        ds = (p * (u - stat_ref[4 + h : 5 + h, :])).astype(BF)
        dvs.append(nn(p.astype(BF), gn_ref[h]).T)
        dks.append(nn(ds, q_ref[h]).T * FACTOR)
        dqt_ref[HD * h : HD * h + HD, :] += nn(kt.astype(BF), ds)
    grad_ref[0, 0:144, :] = jnp.concatenate(dks, axis=0).astype(BF)
    grad_ref[0, 144:288, :] = jnp.concatenate(dvs, axis=0).astype(BF)

    @pl.when(step == pl.num_programs(0) - 1)
    def _():
        rows = (dqt_ref[...] * FACTOR).T
        for s in range(8):
            own = [rows[192 * t + 24 * s : 192 * t + 24 * s + 24] for t in range(4)]
            tail = [own[g // 3][8 * (g % 3) : 8 * (g % 3) + 8, 128:144] for g in range(12)]
            tail = [
                jnp.concatenate(tail[0:8], axis=1),
                jnp.concatenate(tail[8:12] + [jnp.zeros((8, 64), F32)], axis=1),
            ]
            dq_ref[s] = jnp.concatenate([part[:, 0:128] for part in own] + tail, axis=0).astype(BF)


def whole(*shape):
    return pl.BlockSpec(shape, lambda i: (0,) * len(shape))


def block(*shape):
    return pl.BlockSpec((1,) + shape, lambda i: (i,) + (0,) * len(shape))


def on_device(slab_queries, key_tokens, value_tokens, grad_output, out_weight):
    query_rows = slab_queries[0]
    key_rows = key_tokens[0]
    value_rows = value_tokens[0]
    cotangent = grad_output[0]
    v = lax.axis_index("kv")
    swap = [(0, 1), (1, 0)]

    place = jnp.full((1,), v, jnp.int32)
    query_half = lax.dynamic_slice_in_dim(query_rows, 24 * v, 24, 0)
    packed = pl.pallas_call(
        pack_kernel,
        out_shape=jax.ShapeDtypeStruct((8, 304, 256), BF),
        compiler_params=PARAMS,
        name="pack_tokens",
    )(key_rows, value_rows, query_half)
    tokens = lax.all_to_all(packed, CUBE, 0, 0, tiled=True)

    cotangent_half = lax.dynamic_slice_in_dim(cotangent, 384 * v, 384, 0)
    grad_half = lax.dot_general(
        out_weight, cotangent_half, (((1,), (1,)), ((), ())), preferred_element_type=F32
    ).astype(BF)
    grad_four = lax.all_gather(grad_half, "t")
    grad_keep = lax.dynamic_slice_in_dim(grad_four, 2 * v, 2, 0)
    grad_sent = lax.dynamic_slice_in_dim(grad_four, 2 - 2 * v, 2, 0)
    grad_come = lax.ppermute(grad_sent, "kv", swap)

    query_pieces = lax.all_gather(tokens[:, 288:304, :].reshape(128, 256), "t")
    query_pieces = query_pieces.reshape(32, 16, 256)

    stats, attn_turned, queries, grad_heads = pl.pallas_call(
        first_kernel,
        grid=(8,),
        in_specs=[
            SCALAR,
            block(304, 256),
            whole(32, 16, 256),
            whole(2, HD, 384),
            whole(2, HD, 384),
        ],
        out_specs=[
            whole(8, ROWS),
            whole(2, HD, ROWS),
            whole(2, ROWS, HD),
            whole(2, HD, ROWS),
        ],
        out_shape=[
            jax.ShapeDtypeStruct((8, ROWS), F32),
            jax.ShapeDtypeStruct((2, HD, ROWS), F32),
            jax.ShapeDtypeStruct((2, ROWS, HD), BF),
            jax.ShapeDtypeStruct((2, HD, ROWS), BF),
        ],
        scratch_shapes=[pltpu.VMEM((2, ROWS, HD), F32), pltpu.VMEM((2, HD, ROWS), BF)],
        compiler_params=PARAMS_SEQ,
        name="first_pass",
    )(place, tokens, query_pieces, grad_keep, grad_come)

    gathered = lax.all_gather(stats, "t")

    weight_parts = pl.pallas_call(
        weight_kernel,
        out_shape=jax.ShapeDtypeStruct((16, 48, 256), BF),
        compiler_params=PARAMS,
        name="weight_part",
    )(gathered, stats, attn_turned, cotangent)
    weight_come = lax.all_to_all(weight_parts, DP, 0, 0, tiled=True)

    grads, query_grad = pl.pallas_call(
        second_kernel,
        grid=(8,),
        in_specs=[
            block(304, 256),
            whole(2, ROWS, HD),
            whole(2, HD, ROWS),
            whole(4, 8, ROWS),
            ANY,
        ],
        out_specs=[block(288, 256), whole(8, 112, 128)],
        out_shape=[
            jax.ShapeDtypeStruct((8, 288, 256), BF),
            jax.ShapeDtypeStruct((8, 112, 128), BF),
        ],
        scratch_shapes=[
            pltpu.VMEM((2, HD, ROWS), BF),
            pltpu.VMEM((2, ROWS, HD), BF),
            pltpu.VMEM((8, ROWS), F32),
            pltpu.VMEM((144, ROWS), F32),
        ],
        compiler_params=PARAMS_SEQ,
        name="second_pass",
    )(tokens, queries, grad_heads, gathered, weight_parts)

    query_come = lax.all_to_all(query_grad, CUBE, 0, 0, tiled=True)
    weight_keep, weight_sent = pl.pallas_call(
        weight_sum_kernel,
        out_shape=[jax.ShapeDtypeStruct((144, 36), F32)] * 2,
        in_specs=[SCALAR, HERE],
        compiler_params=PARAMS,
        name="weight_sum",
    )(place, weight_come)
    weight_other = lax.ppermute(weight_sent, "kv", swap)
    scattered = pl.pallas_call(
        scatter_kernel,
        out_shape=jax.ShapeDtypeStruct((4, 32, 1152), BF),
        in_specs=[SCALAR, HERE, HERE, HERE],
        compiler_params=PARAMS,
        name="scatter_pack",
    )(place, query_come, weight_keep, weight_other)
    summed = lax.psum_scatter(
        scattered.reshape(128, 1152), "t", scatter_dimension=0, tiled=True
    )
    query_out, weight_out = pl.pallas_call(
        finish_kernel,
        out_shape=[jax.ShapeDtypeStruct((24, 1152), BF), jax.ShapeDtypeStruct((HD, 36), F32)],
        compiler_params=PARAMS,
        cost_estimate=LONG,
        name="finish",
    )(summed)

    grads_back = lax.all_to_all(grads, CUBE, 0, 0, tiled=True)
    key_out, value_out = pl.pallas_call(
        unpack_kernel,
        out_shape=[jax.ShapeDtypeStruct((256, 1152), BF)] * 2,
        in_specs=[HERE, ANY],
        compiler_params=PARAMS,
        name="unpack_grads",
    )(grads_back, weight_out)
    return (key_out[None], value_out[None], query_out[None], weight_out)


def solution(mesh):
    cube = Mesh(mesh.devices.reshape(4, 2, 2, 4, 4, 2), DP + SEQ + ("kv",))
    return jax.shard_map(
        on_device,
        mesh=cube,
        in_specs=(
            P(DP, SEQ, None),
            P(DP, SEQ + ("kv",), None),
            P(DP, SEQ + ("kv",), None),
            P(DP, None, None),
            P(SEQ, None),
        ),
        out_specs=(
            P(DP, SEQ + ("kv",), None),
            P(DP, SEQ + ("kv",), None),
            P(DP, SEQ + ("kv",), None),
            P(SEQ, DP + ("kv",)),
        ),
        check_vma=False,
    )
```

time: 255 us -> 221 us (0.87)
  blocking collectives: 146 us -> 84.5 us
  Pallas kernels: 25.1 us -> 39.1 us
  waiting for transfers between devices: 33.2 us -> 44.7 us
  starting transfers between devices: 26.4 us -> 31.5 us
    all_gather x2 -> x1, blocking collectives: 62.9 us -> 18.9 us  [on_device(): query_pieces = lax.all_gather(tokens[:, 288:304, :].reshape(128, 256), 't')]
    all_to_all x2 -> x0, blocking collectives: 31.4 us -> none  [the longest x1 19.8 us: on_device(): weight_come = lax.all_to_all(weight_turned, DP, 0, 0, tiled=True)]
    reduce_scatter x1, waiting for transfers between devices: 14.8 us -> 41.5 us  [on_device(): lax.psum_scatter(scattered.reshape(128, 1152), 't', scatter_dimension=0,...]
    all_gather x1, blocking collectives: 33.8 us -> 47.1 us  [on_device(): grad_four = lax.all_gather(grad_half, 't')]
    pallas_call x5 -> x7, Pallas kernels: 23.8 us -> 36.5 us  [the longest x1 12.7 us: on_device(): pl.pallas_call(first_kernel, grid=(8,), in_specs=[SCALAR, block(304, 256)...]
    all_to_all x2 -> x3, waiting for transfers between devices: 11.9 us -> 0.01 us  [the longest x1 0.01 us: on_device(): weight_come = lax.all_to_all(weight_parts, DP, 0, 0, tiled=True)]
    all_to_all x2 -> x3, starting transfers between devices: 14.6 us -> 19.4 us  [the longest x1 8.65 us: on_device(): tokens = lax.all_to_all(packed, CUBE, 0, 0, tiled=True)]
    ppermute x1, waiting for transfers between devices: 3.63 us -> 0.01 us  [on_device(): grad_come = lax.ppermute(grad_sent, 'kv', swap)]
  transfers between devices with their start and end apart: 6 -> 7, of which waited for: 4 -> 2; matrix products, arithmetic and copies ran while one was open for 1% -> 1% of each run, Pallas kernels for 0% -> 7%
where the time goes in v2:
time: 221 us; the launch traced here: 220 us
  blocking collectives  84.5 us (38%)
  waiting for transfers between devices  44.7 us (20%)
  Pallas kernels  39.1 us (18%)
  starting transfers between devices  31.5 us (14%)
  between operations  14.1 us (6%)
  local copies, waits for them, and re-layouts  6.01 us (3%)
    all_gather x1, blocking collectives, on_device(): grad_four = lax.all_gather(grad_half, 't')  47.1 us
    reduce_scatter x1, waiting for transfers between devices, on_device(): lax.psum_scatter(scattered.reshape(128, 1152), 't', scatter_dimension=0,...  41.5 us
    all_gather x1, blocking collectives, on_device(): query_pieces = lax.all_gather(tokens[:, 288:304, :].reshape(128, 256), 't')  18.9 us
    all_gather x1, blocking collectives, on_device(): gathered = lax.all_gather(stats, 't')  18.5 us
    pallas_call x1, Pallas kernels, on_device(): pl.pallas_call(first_kernel, grid=(8,), in_specs=[SCALAR, block(304, 256)...  12.7 us
    pallas_call x1, Pallas kernels, on_device(): pl.pallas_call(second_kernel, grid=(8,), in_specs=[block(304, 256), whole...  12.2 us
    all_to_all x1, starting transfers between devices, on_device(): tokens = lax.all_to_all(packed, CUBE, 0, 0, tiled=True)  8.65 us
    all_to_all x1, starting transfers between devices, on_device(): weight_come = lax.all_to_all(weight_parts, DP, 0, 0, tiled=True)  6.54 us
  transfers between devices with their start and end apart: 7, of which 2 were waited for; matrix products, arithmetic and copies ran while one was open for 1% of the time, Pallas kernels for 7%

profile of v2, /device:TPU:64, one launch (start us, length us, event | category | flops | bytes accessed | tf_op | source)
XLA Modules:
  0.0 220.3 jit_solution(9209470941776516700)
XLA Ops:
  7.2 0.0 copy-start
  7.2 1.5 dynamic-slice_bitcast_fusion.q_ref
  8.7 2.8 %pack_tokens.1 = bf16[8,304,256]{2,1,0:T(8,128)(2,1)} custom-call(bf16[256,1152]{1,0:T(8,128)(2,1)} %bitcast.26, bf16[256,1152]{1,0:T(8,128)(2,1)} %bitcast.27, bf16[24,1152]{1,0:T(8,128)(2,1)} %dynamic-slice_bitcast_fusion.q_ref), custom_call_target="tpu_custom_call" | custom-call | tf_op jit(solution)/shard_map/pack_tokens/pallas_call | solution.py:257
  11.5 0.0 copy-start.3
  11.5 8.6 %all-to-all-start = ((bf16[8,304,256]{2,1,0:T(8,128)(2,1)}), bf16[8,304,256]{2,1,0:T(8,128)(2,1)S(1)}, u32[]{:S(2)}, u32[]{:S(2)}) async-start(bf16[8,304,256]{2,1,0:T(8,128)(2,1)} %pack_tokens.1), calls=%async_computation | async-start | bytes 2490368 | tf_op jit(solution)/shard_map/all_to_all | solution.py:263
  20.1 0.0 copy-done
  20.1 0.0 copy-done.3
  20.1 0.4 fusion
  20.6 47.1 %all-gather = bf16[288,384]{1,0:T(8,128)(2,1)S(1)} all-gather(bf16[72,384]{1,0:T(8,128)(2,1)S(1)} %fusion), channel_id=2, replica_groups=mesh['y'=4,'xh'=2,'core'=2,'t'=4,'j'=4,'kv'=2] {'t'}, dimensions={0}, use_global_device_ids=true | all-gather | bytes 276480 | tf_op jit(solution)/shard_map/all_gather | solution.py:269
  67.7 0.7 constant_dynamic-slice_fusion
  68.3 2.8 %collective-permute-start = (bf16[2,72,384]{2,1,0:T(8,128)(2,1)S(1)}, bf16[2,72,384]{2,1,0:T(8,128)(2,1)S(1)}, u32[]{:S(2)}, u32[]{:S(2)}) collective-permute-start(bf16[2,72,384]{2,1,0:T(8,128)(2,1)S(1)} %get-tuple-element.36), channel_id=1, source_target_pairs={{0,1},{1,0},{2,3},{3,2},{4,5},{5,4},{6,7},{7,6},{8,9},{9,8},{10,11... | collective-permute-start | bytes 331784 | tf_op jit(solution)/shard_map/ppermute | solution.py:272
  71.1 0.0 all-to-all-done.kv_ref
  71.2 0.0 copy-start.1
  71.2 18.9 %all_gather.15 = bf16[4,128,256]{2,1,0:T(8,128)(2,1)} all-gather(bf16[1,128,256]{2,1,0:T(8,128)(2,1)S(1)} %bitcast.28), channel_id=1, replica_groups=mesh['y'=4,'xh'=2,'core'=2,'t'=4,'j'=4,'kv'=2] {'t'}, dimensions={0}, use_global_device_ids=true | all-gather | bytes 327680 | tf_op jit(solution)/shard_map/all_gather | solution.py:274
  90.1 0.0 collective-permute-done.come_ref
  90.1 0.0 copy-start.6
  90.1 0.0 copy-done.1
  90.1 0.6 copy-done.6
  90.7 12.7 %first_pass.1 = (f32[8,768]{1,0:T(8,128)}, f32[2,72,768]{2,1,0:T(8,128)}, bf16[2,768,72]{2,1,0:T(8,128)(2,1)}, bf16[2,72,768]{2,1,0:T(8,128)(2,1)}) custom-call(s32[1]{0:T(128)} %bitcast.3.place_ref.v_ref, bf16[8,304,256]{2,1,0:T(8,128)(2,1)} %copy-done.1, bf16[32,16,256]{2,1,0:T(8,128)(2,1)} %bitcast.22, bf16[2,72,384]{2,1,0:T(8,128)(2,1)} %get-tuple-element.37.keep_ref, ...), custom_call_target="tpu_custom_call" | custom-call | tf_op jit(solution)/shard_map/first_pass/pallas_call | solution.py:277
  103.4 18.5 %all-gather.1 = f32[32,768]{1,0:T(8,128)} all-gather(f32[8,768]{1,0:T(8,128)} %get-tuple-element.18.st_ref), channel_id=3, replica_groups=mesh['y'=4,'xh'=2,'core'=2,'t'=4,'j'=4,'kv'=2] {'t'}, dimensions={0}, use_global_device_ids=true | all-gather | bytes 122880 | tf_op jit(solution)/shard_map/all_gather | solution.py:304
  121.9 3.0 %weight_part.1.after_ref = bf16[16,48,256]{2,1,0:T(8,128)(2,1)} custom-call(f32[4,8,768]{2,1,0:T(8,128)} %bitcast.23, f32[8,768]{1,0:T(8,128)} %get-tuple-element.18.st_ref, f32[2,72,768]{2,1,0:T(8,128)} %get-tuple-element.19.ot_ref, bf16[768,1152]{1,0:T(8,128)(2,1)} %bitcast.20), custom_call_target="tpu_custom_call" | custom-call | tf_op jit(solution)/shard_map/weight_part/pallas_call | solution.py:306
  124.9 6.5 %all-to-all-start.3 = ((bf16[16,48,256]{2,1,0:T(8,128)(2,1)}), bf16[16,48,256]{2,1,0:T(8,128)(2,1)S(1)}, u32[]{:S(2)}, u32[]{:S(2)}) async-start(bf16[16,48,256]{2,1,0:T(8,128)(2,1)} %weight_part.1.after_ref), calls=%async_computation.3 | async-start | bytes 786432 | tf_op jit(solution)/shard_map/all_to_all | solution.py:312
  131.5 12.2 %second_pass.1 = (bf16[8,288,256]{2,1,0:T(8,128)(2,1)}, bf16[8,112,128]{2,1,0:T(8,128)(2,1)}) custom-call(bf16[8,304,256]{2,1,0:T(8,128)(2,1)} %copy-done.1, bf16[2,768,72]{2,1,0:T(8,128)(2,1)} %get-tuple-element.16.q_ref, bf16[2,72,768]{2,1,0:T(8,128)(2,1)} %get-tuple-element.17.ga_ref, f32[4,8,768]{2,1,0:T(8,128)} %bitcast.24, ...), custom_call_target="tpu_custom_call" | custom-call | tf_op jit(solution)/shard_map/second_pass/pallas_call | solution.py:314
  143.6 0.0 all-to-all-done.3.w_ref
  143.6 0.0 copy-start.4
  143.7 4.2 %all-to-all-start.2 = ((bf16[8,112,128]{2,1,0:T(8,128)(2,1)}), bf16[8,112,128]{2,1,0:T(8,128)(2,1)S(1)}, u32[]{:S(2)}, u32[]{:S(2)}) async-start(bf16[8,112,128]{2,1,0:T(8,128)(2,1)} %get-tuple-element.21), calls=%async_computation.2 | async-start | bytes 458752 | tf_op jit(solution)/shard_map/all_to_all | solution.py:339
  147.9 0.0 reduce-scatter.2.cloned.1.call-start
  147.9 0.0 copy-done.4
  147.9 1.9 weight_sum.1
  149.8 3.4 %collective-permute-start.1 = (f32[144,36]{1,0:T(8,128)}, f32[144,36]{1,0:T(8,128)S(1)}, u32[]{:S(2)}, u32[]{:S(2)}) collective-permute-start(f32[144,36]{1,0:T(8,128)} %get-tuple-element.23), channel_id=1, source_target_pairs={{0,1},{1,0},{2,3},{3,2},{4,5},{5,4},{6,7},{7,6},{8,9},{9,8},{10,11... | collective-permute-start | bytes 62216 | tf_op jit(solution)/shard_map/ppermute | solution.py:347
  153.1 3.1 %collective-permute-done.1.come_ref = f32[144,36]{1,0:T(8,128)S(1)} collective-permute-done((f32[144,36]{1,0:T(8,128)}, f32[144,36]{1,0:T(8,128)S(1)}, u32[]{:S(2)}, u32[]{:S(2)}) %collective-permute-start.1) | collective-permute-done | bytes 20768 | tf_op jit(solution)/shard_map/ppermute | solution.py:347
  156.3 0.0 copy-start.7
  156.3 0.0 all-to-all-done.2.g_ref
  156.3 0.0 copy-start.5
  156.3 0.6 copy-done.7
  156.9 0.1 copy-done.5
  157.0 2.3 %scatter_pack.1 = bf16[4,32,1152]{2,1,0:T(8,128)(2,1)} custom-call(s32[1]{0:T(128)} %bitcast.3.place_ref.v_ref, bf16[8,112,128]{2,1,0:T(8,128)(2,1)} %copy-done.5, f32[144,36]{1,0:T(8,128)} %get-tuple-element.22.keep_ref, f32[144,36]{1,0:T(8,128)} %copy-done.7), custom_call_target="tpu_custom_call" | custom-call | tf_op jit(solution)/shard_map/scatter_pack/pallas_call | solution.py:348
  159.3 0.0 reduce-scatter.2.cloned.1.call-update
  159.3 6.0 %all-to-all-start.1 = ((bf16[8,288,256]{2,1,0:T(8,128)(2,1)}), bf16[8,288,256]{2,1,0:T(8,128)(2,1)S(1)}, u32[]{:S(2)}, u32[]{:S(2)}) async-start(bf16[8,288,256]{2,1,0:T(8,128)(2,1)} %get-tuple-element.20), calls=%async_computation.1 | async-start | bytes 2359296 | tf_op jit(solution)/shard_map/all_to_all | solution.py:366
  165.3 41.5 %reduce-scatter.2.cloned.1.call-done.x_ref = bf16[32,1152]{1,0:T(8,128)(2,1)} async-done(((bf16[128,1152]{1,0:T(8,128)(2,1)}), bf16[32,1152]{1,0:T(8,128)(2,1)}) %reduce-scatter.2.cloned.1.call-update) | async-done | bytes 73744 | tf_op jit(solution)/shard_map/reduce_scatter | solution.py:355
  206.8 1.6 finish.1
  208.4 1.5 copy.10
  209.9 0.0 all-to-all-done.1.g_ref
  209.9 0.0 copy-start.2
  209.9 1.0 copy-done.2
  210.9 2.5 %unpack_grads.1 = (bf16[256,1152]{1,0:T(8,128)(2,1)}, bf16[256,1152]{1,0:T(8,128)(2,1)}) custom-call(bf16[8,288,256]{2,1,0:T(8,128)(2,1)} %copy-done.2, f32[72,36]{1,0:T(8,128)} %get-tuple-element.35.after_ref), custom_call_target="tpu_custom_call" | custom-call | tf_op jit(solution)/shard_map/unpack_grads/pallas_call | solution.py:367
  (1 shorter events, 0.0 us)
Async XLA Ops:
  7.2 13.0 %copy-start = (bf16[72,1152]{1,0:T(8,128)(2,1)S(1)}, bf16[72,1152]{1,0:T(8,128)(2,1)}, u32[]{:S(2)}) copy-start(bf16[72,1152]{1,0:T(8,128)(2,1)} %param.9) | copy-start | bytes 497668
  11.5 8.7 %copy-start.3 = (bf16[1,768,1152]{2,1,0:T(8,128)(2,1)S(1)}, bf16[1,768,1152]{2,1,0:T(8,128)(2,1)}, u32[]{:S(2)}) copy-start(bf16[1,768,1152]{2,1,0:T(8,128)(2,1)} %param.8) | copy-start | bytes 5308420
  11.5 59.7 %all-to-all-start = ((bf16[8,304,256]{2,1,0:T(8,128)(2,1)}), bf16[8,304,256]{2,1,0:T(8,128)(2,1)S(1)}, u32[]{:S(2)}, u32[]{:S(2)}) async-start(bf16[8,304,256]{2,1,0:T(8,128)(2,1)} %pack_tokens.1), calls=%async_computation | async-start | bytes 2490368 | tf_op jit(solution)/shard_map/all_to_all | solution.py:263
  68.3 21.7 %collective-permute-start = (bf16[2,72,384]{2,1,0:T(8,128)(2,1)S(1)}, bf16[2,72,384]{2,1,0:T(8,128)(2,1)S(1)}, u32[]{:S(2)}, u32[]{:S(2)}) collective-permute-start(bf16[2,72,384]{2,1,0:T(8,128)(2,1)S(1)} %get-tuple-element.36), channel_id=1, source_target_pairs={{0,1},{1,0},{2,3},{3,2},{4,5},{5,4},{6,7},{7,6},{8,9},{9,8},{10,11... | collective-permute-start | bytes 331784 | tf_op jit(solution)/shard_map/ppermute | solution.py:272
  71.2 18.9 %copy-start.1 = (bf16[8,304,256]{2,1,0:T(8,128)(2,1)}, bf16[8,304,256]{2,1,0:T(8,128)(2,1)S(1)}, u32[]{:S(2)}) copy-start(bf16[8,304,256]{2,1,0:T(8,128)(2,1)S(1)} %all-to-all-done.kv_ref) | copy-start | bytes 3735556
  90.1 0.6 copy-start.6
  124.9 18.7 %all-to-all-start.3 = ((bf16[16,48,256]{2,1,0:T(8,128)(2,1)}), bf16[16,48,256]{2,1,0:T(8,128)(2,1)S(1)}, u32[]{:S(2)}, u32[]{:S(2)}) async-start(bf16[16,48,256]{2,1,0:T(8,128)(2,1)} %weight_part.1.after_ref), calls=%async_computation.3 | async-start | bytes 786432 | tf_op jit(solution)/shard_map/all_to_all | solution.py:312
  143.6 4.2 %copy-start.4 = (bf16[16,48,256]{2,1,0:T(8,128)(2,1)}, bf16[16,48,256]{2,1,0:T(8,128)(2,1)S(1)}, u32[]{:S(2)}) copy-start(bf16[16,48,256]{2,1,0:T(8,128)(2,1)S(1)} %all-to-all-done.3.w_ref) | copy-start | bytes 1179652
  143.7 12.6 %all-to-all-start.2 = ((bf16[8,112,128]{2,1,0:T(8,128)(2,1)}), bf16[8,112,128]{2,1,0:T(8,128)(2,1)S(1)}, u32[]{:S(2)}, u32[]{:S(2)}) async-start(bf16[8,112,128]{2,1,0:T(8,128)(2,1)} %get-tuple-element.21), calls=%async_computation.2 | async-start | bytes 458752 | tf_op jit(solution)/shard_map/all_to_all | solution.py:339
  147.9 59.0 %reduce-scatter.2.cloned.1.call-start = ((), (), s32[]{:S(2)}) async-start(), calls=%async_computation.5 | async-start | bytes 368640 | tf_op jit(solution)/shard_map/reduce_scatter | solution.py:355
  149.8 6.5 %collective-permute-start.1 = (f32[144,36]{1,0:T(8,128)}, f32[144,36]{1,0:T(8,128)S(1)}, u32[]{:S(2)}, u32[]{:S(2)}) collective-permute-start(f32[144,36]{1,0:T(8,128)} %get-tuple-element.23), channel_id=1, source_target_pairs={{0,1},{1,0},{2,3},{3,2},{4,5},{5,4},{6,7},{7,6},{8,9},{9,8},{10,11... | collective-permute-start | bytes 62216 | tf_op jit(solution)/shard_map/ppermute | solution.py:347
  156.3 0.6 copy-start.7
  156.3 0.7 copy-start.5
  159.3 50.5 %all-to-all-start.1 = ((bf16[8,288,256]{2,1,0:T(8,128)(2,1)}), bf16[8,288,256]{2,1,0:T(8,128)(2,1)S(1)}, u32[]{:S(2)}, u32[]{:S(2)}) async-start(bf16[8,288,256]{2,1,0:T(8,128)(2,1)} %get-tuple-element.20), calls=%async_computation.1 | async-start | bytes 2359296 | tf_op jit(solution)/shard_map/all_to_all | solution.py:366
  209.9 1.0 copy-start.2
Sparse Core Ops, SparseCore 0:
  159.5 47.3 reduce-scatter.1

commit v3 on v2

v3 whole, which is shorter than its diff:
```python
import math

import jax
import jax.numpy as jnp
from jax import lax
from jax.experimental import pallas as pl
from jax.experimental.pallas import tpu as pltpu
from jax.sharding import Mesh
from jax.sharding import PartitionSpec as P

HD = 72
ROWS = 768
FACTOR = 1.0 / math.sqrt(HD)
SCALE = FACTOR * math.log2(math.e)
BF = jnp.bfloat16
F32 = jnp.float32
VMEM = 60 * 1024 * 1024
LONG = pl.CostEstimate(flops=60_000_000_000, bytes_accessed=200_000_000, transcendentals=0)
ANY = pl.BlockSpec(memory_space=pl.ANY)
SCALAR = pl.BlockSpec(memory_space=pltpu.SMEM)
HERE = pl.BlockSpec(memory_space=pltpu.VMEM)
CUBE = ("j", "kv")
DP = ("y", "xh", "core")
SEQ = ("t", "j")
PARAMS = pltpu.CompilerParams(vmem_limit_bytes=VMEM)


def heads_of(place):
    j, v = place // 2, place % 2
    return (8 * v + j, 8 * v + 4 + j)


def nn(a, b):
    return lax.dot_general(a, b, (((1,), (0,)), ((), ())), preferred_element_type=F32)


def minus_parts(x):
    first = (-x).astype(BF)
    rest = -x - first.astype(F32)
    second = rest.astype(BF)
    third = (rest - second.astype(F32)).astype(BF)
    zeros = jnp.zeros((5,) + x.shape[1:], F32)
    return jnp.concatenate(
        [first.astype(F32), second.astype(F32), third.astype(F32), zeros], axis=0
    ).astype(BF)


def with_ones(x):
    row = lax.broadcasted_iota(jnp.int32, (8, x.shape[1]), 0)
    return jnp.concatenate([x, jnp.where(row < 3, 1.0, 0.0)], axis=0)


def pack_kernel(half_ref, k_ref, v_ref, q_ref, o_ref):
    every = q_ref[...].astype(F32)
    rows = jnp.where(half_ref[0] == 0, every[0:24], every[24:48])
    for first, ref in ((0, k_ref), (144, v_ref)):
        turned = ref[...].astype(F32).T
        for place in range(8):
            a, b = heads_of(place)
            o_ref[place, first : first + 144, :] = jnp.concatenate(
                [turned[HD * a : HD * a + HD], turned[HD * b : HD * b + HD]], axis=0
            ).astype(BF)
    for place in range(8):
        a, b = heads_of(place)
        qa = rows[:, HD * a : HD * a + HD]
        qb = rows[:, HD * b : HD * b + HD]
        middle = jnp.concatenate([qa[16:24], qb[0:8]], axis=0)
        o_ref[place, 288:304, :] = jnp.concatenate(
            [qa[0:16], middle, qb[8:24], jnp.zeros((16, 40), F32)], axis=1
        ).astype(BF)


def scatter_kernel(g_ref, w_ref, o_ref):
    heads = [None] * 16
    for place in range(8):
        piece = g_ref[place].astype(F32)
        tail = jnp.concatenate(
            [
                piece[96 + 8 * (g // 8) : 104 + 8 * (g // 8), 16 * (g % 8) : 16 * (g % 8) + 16]
                for g in range(12)
            ],
            axis=0,
        )
        a, b = heads_of(place)
        heads[a] = piece[0:96, 0:72]
        heads[b] = jnp.concatenate([piece[0:96, 72:128], tail], axis=1)
    rows = jnp.concatenate(heads, axis=1)
    for v in range(2):
        total = jnp.zeros((48, 128), F32)
        for source in range(16):
            total = total + w_ref[2 * source + v].astype(F32)
        weight = jnp.concatenate([total[:, 36 * k : 36 * k + 36] for k in range(3)], axis=0)
        for i in range(2):
            t = 2 * v + i
            folded = [weight[HD * i + 8 * k : HD * i + 8 * k + 8] for k in range(9)]
            folded = jnp.concatenate(folded + [jnp.zeros((8, 828), F32)], axis=1)
            o_ref[t] = jnp.concatenate([rows[24 * t : 24 * t + 24], folded], axis=0).astype(BF)


def finish_kernel(x_ref, q_ref, w_ref):
    q_ref[...] = x_ref[0:24, :]
    folded = x_ref[...].astype(F32)[24:32]
    weight = jnp.concatenate([folded[:, 36 * k : 36 * k + 36] for k in range(9)], axis=0)
    w_ref[...] = weight.T


def unpack_kernel(g_ref, after_ref, k_ref, v_ref):
    for part, o_ref in ((0, k_ref), (1, v_ref)):
        heads = [None] * 16
        for place in range(8):
            block = g_ref[place, 144 * part : 144 * part + 144, :].astype(F32)
            a, b = heads_of(place)
            heads[a] = block[0:HD]
            heads[b] = block[HD : 2 * HD]
        o_ref[...] = jnp.concatenate(heads, axis=0).T.astype(BF)


def first_kernel(
    half_ref, kv_ref, qg_ref, keep_ref, come_ref, st_ref, ot_ref, q_ref, ga_ref, qs_ref, qt_ref, kh_ref
):
    for block in range(32):
        piece = qg_ref[block].astype(F32)
        base = 24 * block
        qs_ref[0, base : base + 16, :] = piece[:, 0:72]
        qs_ref[0, base + 16 : base + 24, :] = piece[0:8, 72:144]
        qs_ref[1, base : base + 8, :] = piece[8:16, 72:144]
        qs_ref[1, base + 8 : base + 24, :] = piece[:, 144:216]

    @pl.when(half_ref[0] == 0)
    def _():
        ga_ref[:, :, 0:384] = keep_ref[...]
        ga_ref[:, :, 384:768] = come_ref[...]

    @pl.when(half_ref[0] == 1)
    def _():
        ga_ref[:, :, 0:384] = come_ref[...]
        ga_ref[:, :, 384:768] = keep_ref[...]

    for h in range(2):
        q_ref[h] = qs_ref[h].astype(BF)
        qt_ref[h, 0:72] = qs_ref[h].T.astype(BF)
    st_ref[0:2, :] = jnp.full((2, ROWS), -1e30, F32)
    st_ref[2:8, :] = jnp.zeros((6, ROWS), F32)
    ot_ref[...] = jnp.zeros_like(ot_ref)

    for i in range(8):
        keys = kv_ref[i, 0:144, :].astype(F32)
        for h in range(2):
            kh = with_ones(keys[HD * h : HD * h + HD]).T.astype(BF)
            kh_ref[h, i] = kh
            s = nn(kh[:, 0:72], qt_ref[h, 0:72])
            st_ref[h : h + 1, :] = jnp.maximum(
                st_ref[h : h + 1, :], jnp.max(s, axis=0, keepdims=True)
            )
    for h in range(2):
        qt_ref[h, 72:80] = minus_parts(st_ref[h : h + 1, :])
    for i in range(8):
        values = kv_ref[i, 144:288, :].astype(F32)
        for h in range(2):
            vt = values[HD * h : HD * h + HD]
            u = nn(vt.T.astype(BF), ga_ref[h])
            e = jnp.exp2(nn(kh_ref[h, i], qt_ref[h]) * SCALE)
            st_ref[2 + h : 3 + h, :] += jnp.sum(e, axis=0, keepdims=True)
            st_ref[4 + h : 5 + h, :] += jnp.sum(e * u, axis=0, keepdims=True)
            ot_ref[h] += nn(vt.astype(BF), e.astype(BF))


def joined(sg_ref, h):
    tops = [sg_ref[t, h : h + 1, :] for t in range(4)]
    highest = jnp.maximum(jnp.maximum(tops[0], tops[1]), jnp.maximum(tops[2], tops[3]))
    total = jnp.zeros((1, ROWS), F32)
    weighted = jnp.zeros((1, ROWS), F32)
    for t in range(4):
        part = jnp.exp2((tops[t] - highest) * SCALE)
        total = total + sg_ref[t, 2 + h : 3 + h, :] * part
        weighted = weighted + sg_ref[t, 4 + h : 5 + h, :] * part
    return highest, total, weighted / total


def weight_kernel(sg_ref, st_ref, ot_ref, go_ref, o_ref):
    rows = []
    for h in range(2):
        highest, total, _ = joined(sg_ref, h)
        share = jnp.exp2((st_ref[h : h + 1, :] - highest) * SCALE) / total
        rows.append(ot_ref[h] * share)
    attn = jnp.concatenate(rows, axis=0).astype(BF)
    product = nn(attn, go_ref[...])
    for c in range(32):
        part = product[:, 36 * c : 36 * c + 36]
        o_ref[c] = jnp.concatenate(
            [part[0:48], part[48:96], part[96:144], jnp.zeros((48, 20), F32)], axis=1
        ).astype(BF)


def second_kernel(
    kv_ref, q_ref, ga_ref, sg_ref, after_ref, grad_ref, dq_ref, qt_ref, gt_ref, gn_ref, dqt_ref
):
    for h in range(2):
        highest, total, delta = joined(sg_ref, h)
        level = highest + jnp.log2(total) * (1.0 / SCALE)
        qt_ref[h, 0:72] = q_ref[h].astype(F32).T.astype(BF)
        qt_ref[h, 72:80] = minus_parts(level)
        grads = ga_ref[h].astype(F32)
        gt_ref[h, 0:72] = ga_ref[h]
        gt_ref[h, 72:80] = minus_parts(delta)
        gn_ref[h] = grads.T.astype(BF)
    dqt_ref[...] = jnp.zeros_like(dqt_ref)

    for i in range(8):
        keys = kv_ref[i, 0:144, :].astype(F32)
        values = kv_ref[i, 144:288, :].astype(F32)
        dks, dvs = [], []
        for h in range(2):
            kt = keys[HD * h : HD * h + HD]
            kh = with_ones(kt).T.astype(BF)
            vh = with_ones(values[HD * h : HD * h + HD]).T.astype(BF)
            p = jnp.exp2(nn(kh, qt_ref[h]) * SCALE)
            ds = (p * nn(vh, gt_ref[h])).astype(BF)
            dvs.append(nn(p.astype(BF), gn_ref[h]).T)
            dks.append(nn(ds, q_ref[h]).T * FACTOR)
            dqt_ref[HD * h : HD * h + HD, :] += nn(kt.astype(BF), ds)
        grad_ref[i, 0:144, :] = jnp.concatenate(dks, axis=0).astype(BF)
        grad_ref[i, 144:288, :] = jnp.concatenate(dvs, axis=0).astype(BF)

    rows = (dqt_ref[...] * FACTOR).T
    for s in range(8):
        own = [rows[192 * t + 24 * s : 192 * t + 24 * s + 24] for t in range(4)]
        tail = [own[g // 3][8 * (g % 3) : 8 * (g % 3) + 8, 128:144] for g in range(12)]
        tail = [
            jnp.concatenate(tail[0:8], axis=1),
            jnp.concatenate(tail[8:12] + [jnp.zeros((8, 64), F32)], axis=1),
        ]
        dq_ref[s] = jnp.concatenate([part[:, 0:128] for part in own] + tail, axis=0).astype(BF)


def on_device(slab_queries, key_tokens, value_tokens, grad_output, out_weight):
    query_rows = slab_queries[0]
    key_rows = key_tokens[0]
    value_rows = value_tokens[0]
    cotangent = grad_output[0]
    v = lax.axis_index("kv")
    swap = [(0, 1), (1, 0)]

    place = jnp.full((1,), v, jnp.int32)
    packed = pl.pallas_call(
        pack_kernel,
        out_shape=jax.ShapeDtypeStruct((8, 304, 256), BF),
        in_specs=[SCALAR, HERE, HERE, HERE],
        compiler_params=PARAMS,
        name="pack_tokens",
    )(place, key_rows, value_rows, query_rows)
    tokens = lax.all_to_all(packed, CUBE, 0, 0, tiled=True)

    cotangent_half = lax.dynamic_slice_in_dim(cotangent, 384 * v, 384, 0)
    grad_half = lax.dot_general(
        out_weight, cotangent_half, (((1,), (1,)), ((), ())), preferred_element_type=F32
    ).astype(BF)
    grad_four = lax.all_gather(grad_half, "t")
    grad_keep = lax.dynamic_slice_in_dim(grad_four, 2 * v, 2, 0)
    grad_sent = lax.dynamic_slice_in_dim(grad_four, 2 - 2 * v, 2, 0)
    grad_come = lax.ppermute(grad_sent, "kv", swap)

    query_pieces = lax.all_gather(tokens[:, 288:304, :].reshape(128, 256), "t")
    query_pieces = query_pieces.reshape(32, 16, 256)

    stats, attn_turned, queries, grad_heads = pl.pallas_call(
        first_kernel,
        in_specs=[SCALAR, HERE, HERE, HERE, HERE],
        out_shape=[
            jax.ShapeDtypeStruct((8, ROWS), F32),
            jax.ShapeDtypeStruct((2, HD, ROWS), F32),
            jax.ShapeDtypeStruct((2, ROWS, HD), BF),
            jax.ShapeDtypeStruct((2, HD, ROWS), BF),
        ],
        scratch_shapes=[
            pltpu.VMEM((2, ROWS, HD), F32),
            pltpu.VMEM((2, 80, ROWS), BF),
            pltpu.VMEM((2, 8, 256, 80), BF),
        ],
        compiler_params=PARAMS,
        name="first_pass",
    )(place, tokens, query_pieces, grad_keep, grad_come)

    gathered = lax.all_gather(stats, "t")

    weight_parts = pl.pallas_call(
        weight_kernel,
        out_shape=jax.ShapeDtypeStruct((32, 48, 128), BF),
        compiler_params=PARAMS,
        name="weight_part",
    )(gathered, stats, attn_turned, cotangent)
    weight_come = lax.all_to_all(weight_parts, DP + ("kv",), 0, 0, tiled=True)

    grads, query_grad = pl.pallas_call(
        second_kernel,
        in_specs=[HERE, HERE, HERE, HERE, ANY],
        out_shape=[
            jax.ShapeDtypeStruct((8, 288, 256), BF),
            jax.ShapeDtypeStruct((8, 112, 128), BF),
        ],
        scratch_shapes=[
            pltpu.VMEM((2, 80, ROWS), BF),
            pltpu.VMEM((2, 80, ROWS), BF),
            pltpu.VMEM((2, ROWS, HD), BF),
            pltpu.VMEM((144, ROWS), F32),
        ],
        compiler_params=PARAMS,
        name="second_pass",
    )(tokens, queries, grad_heads, gathered, weight_parts)

    query_come = lax.all_to_all(query_grad, CUBE, 0, 0, tiled=True)
    scattered = pl.pallas_call(
        scatter_kernel,
        out_shape=jax.ShapeDtypeStruct((4, 32, 1152), BF),
        compiler_params=PARAMS,
        name="scatter_pack",
    )(query_come, weight_come)
    summed = lax.psum_scatter(
        scattered.reshape(128, 1152), "t", scatter_dimension=0, tiled=True
    )
    query_out, weight_out = pl.pallas_call(
        finish_kernel,
        out_shape=[jax.ShapeDtypeStruct((24, 1152), BF), jax.ShapeDtypeStruct((36, HD), F32)],
        compiler_params=PARAMS,
        cost_estimate=LONG,
        name="finish",
    )(summed)

    grads_back = lax.all_to_all(grads, CUBE, 0, 0, tiled=True)
    key_out, value_out = pl.pallas_call(
        unpack_kernel,
        out_shape=[jax.ShapeDtypeStruct((256, 1152), BF)] * 2,
        in_specs=[HERE, ANY],
        compiler_params=PARAMS,
        name="unpack_grads",
    )(grads_back, weight_out)
    return (key_out[None], value_out[None], query_out[None], weight_out.T)


def solution(mesh):
    cube = Mesh(mesh.devices.reshape(4, 2, 2, 4, 4, 2), DP + SEQ + ("kv",))
    return jax.shard_map(
        on_device,
        mesh=cube,
        in_specs=(
            P(DP, SEQ, None),
            P(DP, SEQ + ("kv",), None),
            P(DP, SEQ + ("kv",), None),
            P(DP, None, None),
            P(SEQ, None),
        ),
        out_specs=(
            P(DP, SEQ + ("kv",), None),
            P(DP, SEQ + ("kv",), None),
            P(DP, SEQ + ("kv",), None),
            P(SEQ, DP + ("kv",)),
        ),
        check_vma=False,
    )
```

time: 221 us -> 214 us (0.968)
  blocking collectives: 84.5 us -> 96.7 us
  starting transfers between devices: 31.5 us -> 24.1 us
  Pallas kernels: 39.1 us -> 33.6 us
  local copies, waits for them, and re-layouts: 6.01 us -> 2.39 us
  waiting for transfers between devices: 44.7 us -> 42.3 us
    all_to_all x0 -> x1, blocking collectives: none -> 12.2 us  [on_device(): query_come = lax.all_to_all(query_grad, CUBE, 0, 0, tiled=True)]
    pallas_call x4 -> x3, Pallas kernels: 29.8 us -> 24.1 us  [the longest x1 10.7 us: on_device(): pl.pallas_call(first_kernel, in_specs=[SCALAR, HERE, HERE, HERE, HERE], o...]
    all_to_all x2 -> x1, starting transfers between devices: 10.8 us -> 6.87 us  [on_device(): weight_come = lax.all_to_all(weight_parts, DP + ('kv',), 0, 0, tiled=True)]
    ppermute x1 -> x0, starting transfers between devices: 3.36 us -> none  [on_device(): weight_other = lax.ppermute(weight_sent, 'kv', swap)]
    ppermute x1 -> x0, waiting for transfers between devices: 3.12 us -> none  [on_device(): weight_other = lax.ppermute(weight_sent, 'kv', swap)]
  transfers between devices with their start and end apart: 7 -> 5, of which waited for: 2 -> 1; matrix products, arithmetic and copies ran while one was open for 1% -> 1% of each run, Pallas kernels for 7% -> 6%
where the time goes in v3:
time: 214 us; the launch traced here: 213 us
  blocking collectives  96.7 us (45%)
  waiting for transfers between devices  42.3 us (20%)
  Pallas kernels  33.6 us (16%)
  starting transfers between devices  24.1 us (11%)
  between operations  14.1 us (7%)
  local copies, waits for them, and re-layouts  2.39 us (1%)
    all_gather x1, blocking collectives, on_device(): grad_four = lax.all_gather(grad_half, 't')  47.1 us
    reduce_scatter x1, waiting for transfers between devices, on_device(): lax.psum_scatter(scattered.reshape(128, 1152), 't', scatter_dimension=0,...  42.2 us
    all_gather x1, blocking collectives, on_device(): query_pieces = lax.all_gather(tokens[:, 288:304, :].reshape(128, 256), 't')  18.9 us
    all_gather x1, blocking collectives, on_device(): gathered = lax.all_gather(stats, 't')  18.4 us
    all_to_all x1, blocking collectives, on_device(): query_come = lax.all_to_all(query_grad, CUBE, 0, 0, tiled=True)  12.2 us
    pallas_call x1, Pallas kernels, on_device(): pl.pallas_call(first_kernel, in_specs=[SCALAR, HERE, HERE, HERE, HERE], o...  10.7 us
    pallas_call x1, Pallas kernels, on_device(): pl.pallas_call(second_kernel, in_specs=[HERE, HERE, HERE, HERE, ANY], out...  10.2 us
    all_to_all x1, starting transfers between devices, on_device(): tokens = lax.all_to_all(packed, CUBE, 0, 0, tiled=True)  8.65 us
  transfers between devices with their start and end apart: 5, of which 1 were waited for; matrix products, arithmetic and copies ran while one was open for 1% of the time, Pallas kernels for 6%

profile of v3, /device:TPU:64, one launch (start us, length us, event | category | flops | bytes accessed | tf_op | source)
XLA Modules:
  0.0 213.5 jit_solution(2346563568001595269)
XLA Ops:
  7.2 0.0 copy-start
  7.2 2.8 %pack_tokens.1 = bf16[8,304,256]{2,1,0:T(8,128)(2,1)} custom-call(s32[1]{0:T(128)} %bitcast.half_ref, bf16[256,1152]{1,0:T(8,128)(2,1)} %bitcast.26, bf16[256,1152]{1,0:T(8,128)(2,1)} %bitcast.27, bf16[48,1152]{1,0:T(8,128)(2,1)} %bitcast.29), custom_call_target="tpu_custom_call" | custom-call | tf_op jit(solution)/shard_map/pack_tokens/pallas_call | solution.py:245
  10.0 0.0 copy-start.3
  10.0 8.6 %all-to-all-start = ((bf16[8,304,256]{2,1,0:T(8,128)(2,1)}), bf16[8,304,256]{2,1,0:T(8,128)(2,1)S(1)}, u32[]{:S(2)}, u32[]{:S(2)}) async-start(bf16[8,304,256]{2,1,0:T(8,128)(2,1)} %pack_tokens.1), calls=%async_computation | async-start | bytes 2490368 | tf_op jit(solution)/shard_map/all_to_all | solution.py:252
  18.7 0.0 copy-done
  18.7 0.0 copy-done.3
  18.7 0.4 fusion
  19.1 47.1 %all-gather = bf16[288,384]{1,0:T(8,128)(2,1)S(1)} all-gather(bf16[72,384]{1,0:T(8,128)(2,1)S(1)} %fusion), channel_id=2, replica_groups=mesh['y'=4,'xh'=2,'core'=2,'t'=4,'j'=4,'kv'=2] {'t'}, dimensions={0}, use_global_device_ids=true | all-gather | bytes 276480 | tf_op jit(solution)/shard_map/all_gather | solution.py:258
  66.2 0.7 constant_dynamic-slice_fusion
  66.9 2.8 %collective-permute-start = (bf16[2,72,384]{2,1,0:T(8,128)(2,1)S(1)}, bf16[2,72,384]{2,1,0:T(8,128)(2,1)S(1)}, u32[]{:S(2)}, u32[]{:S(2)}) collective-permute-start(bf16[2,72,384]{2,1,0:T(8,128)(2,1)S(1)} %get-tuple-element.24), channel_id=1, source_target_pairs={{0,1},{1,0},{2,3},{3,2},{4,5},{5,4},{6,7},{7,6},{8,9},{9,8},{10,11... | collective-permute-start | bytes 331784 | tf_op jit(solution)/shard_map/ppermute | solution.py:261
  69.7 0.0 all-to-all-done.kv_ref
  69.7 0.0 copy-start.1
  69.7 18.9 %all_gather.15 = bf16[4,128,256]{2,1,0:T(8,128)(2,1)} all-gather(bf16[1,128,256]{2,1,0:T(8,128)(2,1)S(1)} %bitcast.28), channel_id=1, replica_groups=mesh['y'=4,'xh'=2,'core'=2,'t'=4,'j'=4,'kv'=2] {'t'}, dimensions={0}, use_global_device_ids=true | all-gather | bytes 327680 | tf_op jit(solution)/shard_map/all_gather | solution.py:263
  88.6 0.0 collective-permute-done.come_ref
  88.6 0.0 copy-start.5
  88.6 0.0 copy-done.1
  88.6 0.6 copy-done.5
  89.3 10.7 %first_pass.1 = (f32[8,768]{1,0:T(8,128)}, f32[2,72,768]{2,1,0:T(8,128)}, bf16[2,768,72]{2,1,0:T(8,128)(2,1)}, bf16[2,72,768]{2,1,0:T(8,128)(2,1)}) custom-call(s32[1]{0:T(128)} %bitcast.half_ref, bf16[8,304,256]{2,1,0:T(8,128)(2,1)} %copy-done.1, bf16[32,16,256]{2,1,0:T(8,128)(2,1)} %bitcast.22, bf16[2,72,384]{2,1,0:T(8,128)(2,1)} %get-tuple-element.25.keep_ref, ...), custom_call_target="tpu_custom_call" | custom-call | tf_op jit(solution)/shard_map/first_pass/pallas_call | solution.py:266
  100.0 18.4 %all-gather.1 = f32[32,768]{1,0:T(8,128)} all-gather(f32[8,768]{1,0:T(8,128)} %get-tuple-element.16.st_ref), channel_id=3, replica_groups=mesh['y'=4,'xh'=2,'core'=2,'t'=4,'j'=4,'kv'=2] {'t'}, dimensions={0}, use_global_device_ids=true | all-gather | bytes 122880 | tf_op jit(solution)/shard_map/all_gather | solution.py:284
  118.4 3.2 %weight_part.1.after_ref = bf16[32,48,128]{2,1,0:T(8,128)(2,1)} custom-call(f32[4,8,768]{2,1,0:T(8,128)} %bitcast.23, f32[8,768]{1,0:T(8,128)} %get-tuple-element.16.st_ref, f32[2,72,768]{2,1,0:T(8,128)} %get-tuple-element.17.ot_ref, bf16[768,1152]{1,0:T(8,128)(2,1)} %bitcast.20), custom_call_target="tpu_custom_call" | custom-call | tf_op jit(solution)/shard_map/weight_part/pallas_call | solution.py:286
  121.6 6.9 %all-to-all-start.3 = ((bf16[32,48,128]{2,1,0:T(8,128)(2,1)}), bf16[32,48,128]{2,1,0:T(8,128)(2,1)S(1)}, u32[]{:S(2)}, u32[]{:S(2)}) async-start(bf16[32,48,128]{2,1,0:T(8,128)(2,1)} %weight_part.1.after_ref), calls=%async_computation.3 | async-start | bytes 786432 | tf_op jit(solution)/shard_map/all_to_all | solution.py:292
  128.4 0.2 reduce-scatter.2.cloned.1.call-start
  128.7 10.2 %second_pass.1 = (bf16[8,288,256]{2,1,0:T(8,128)(2,1)}, bf16[8,112,128]{2,1,0:T(8,128)(2,1)}) custom-call(bf16[8,304,256]{2,1,0:T(8,128)(2,1)} %copy-done.1, bf16[2,768,72]{2,1,0:T(8,128)(2,1)} %get-tuple-element.14.q_ref, bf16[2,72,768]{2,1,0:T(8,128)(2,1)} %get-tuple-element.15.ga_ref, f32[4,8,768]{2,1,0:T(8,128)} %bitcast.24, ...), custom_call_target="tpu_custom_call" | custom-call | tf_op jit(solution)/shard_map/second_pass/pallas_call | solution.py:294
  138.9 0.0 all-to-all-done.3.w_ref
  138.9 0.0 copy-start.4
  138.9 12.2 %all_to_all.20.g_ref = bf16[8,112,128]{2,1,0:T(8,128)(2,1)} all-to-all(bf16[8,112,128]{2,1,0:T(8,128)(2,1)} %get-tuple-element.19), channel_id=1, replica_groups=mesh['y'=4,'xh'=2,'core'=2,'t'=4,'j'=4,'kv'=2] {'j','kv'}, dimensions={0} | all-to-all | bytes 458752 | tf_op jit(solution)/shard_map/all_to_all | solution.py:311
  151.1 0.0 copy-done.4
  151.1 2.5 %scatter_pack.1 = bf16[4,32,1152]{2,1,0:T(8,128)(2,1)} custom-call(bf16[8,112,128]{2,1,0:T(8,128)(2,1)} %all_to_all.20.g_ref, bf16[32,48,128]{2,1,0:T(8,128)(2,1)} %copy-done.4), custom_call_target="tpu_custom_call" | custom-call | tf_op jit(solution)/shard_map/scatter_pack/pallas_call | solution.py:312
  153.6 0.0 reduce-scatter.2.cloned.1.call-update
  153.7 5.5 %all-to-all-start.1 = ((bf16[8,288,256]{2,1,0:T(8,128)(2,1)}), bf16[8,288,256]{2,1,0:T(8,128)(2,1)S(1)}, u32[]{:S(2)}, u32[]{:S(2)}) async-start(bf16[8,288,256]{2,1,0:T(8,128)(2,1)} %get-tuple-element.18), calls=%async_computation.1 | async-start | bytes 2359296 | tf_op jit(solution)/shard_map/all_to_all | solution.py:329
  159.2 42.2 %reduce-scatter.2.cloned.1.call-done.x_ref = bf16[32,1152]{1,0:T(8,128)(2,1)} async-done(((bf16[128,1152]{1,0:T(8,128)(2,1)}), bf16[32,1152]{1,0:T(8,128)(2,1)}) %reduce-scatter.2.cloned.1.call-update) | async-done | bytes 73744 | tf_op jit(solution)/shard_map/reduce_scatter | solution.py:318
  201.4 1.6 finish.1
  203.1 0.0 all-to-all-done.1.g_ref
  203.1 0.0 copy-start.2
  203.1 1.1 copy-done.2
  204.1 2.5 %unpack_grads.1 = (bf16[256,1152]{1,0:T(8,128)(2,1)}, bf16[256,1152]{1,0:T(8,128)(2,1)}) custom-call(bf16[8,288,256]{2,1,0:T(8,128)(2,1)} %copy-done.2, f32[36,72]{1,0:T(8,128)} %get-tuple-element.20.after_ref), custom_call_target="tpu_custom_call" | custom-call | tf_op jit(solution)/shard_map/unpack_grads/pallas_call | solution.py:330
  (1 shorter events, 0.0 us)
Async XLA Ops:
  7.2 11.5 %copy-start = (bf16[72,1152]{1,0:T(8,128)(2,1)S(1)}, bf16[72,1152]{1,0:T(8,128)(2,1)}, u32[]{:S(2)}) copy-start(bf16[72,1152]{1,0:T(8,128)(2,1)} %param.9) | copy-start | bytes 497668
  10.0 8.7 %copy-start.3 = (bf16[1,768,1152]{2,1,0:T(8,128)(2,1)S(1)}, bf16[1,768,1152]{2,1,0:T(8,128)(2,1)}, u32[]{:S(2)}) copy-start(bf16[1,768,1152]{2,1,0:T(8,128)(2,1)} %param.8) | copy-start | bytes 5308420
  10.0 59.6 %all-to-all-start = ((bf16[8,304,256]{2,1,0:T(8,128)(2,1)}), bf16[8,304,256]{2,1,0:T(8,128)(2,1)S(1)}, u32[]{:S(2)}, u32[]{:S(2)}) async-start(bf16[8,304,256]{2,1,0:T(8,128)(2,1)} %pack_tokens.1), calls=%async_computation | async-start | bytes 2490368 | tf_op jit(solution)/shard_map/all_to_all | solution.py:252
  66.9 21.7 %collective-permute-start = (bf16[2,72,384]{2,1,0:T(8,128)(2,1)S(1)}, bf16[2,72,384]{2,1,0:T(8,128)(2,1)S(1)}, u32[]{:S(2)}, u32[]{:S(2)}) collective-permute-start(bf16[2,72,384]{2,1,0:T(8,128)(2,1)S(1)} %get-tuple-element.24), channel_id=1, source_target_pairs={{0,1},{1,0},{2,3},{3,2},{4,5},{5,4},{6,7},{7,6},{8,9},{9,8},{10,11... | collective-permute-start | bytes 331784 | tf_op jit(solution)/shard_map/ppermute | solution.py:261
  69.7 18.9 %copy-start.1 = (bf16[8,304,256]{2,1,0:T(8,128)(2,1)}, bf16[8,304,256]{2,1,0:T(8,128)(2,1)S(1)}, u32[]{:S(2)}) copy-start(bf16[8,304,256]{2,1,0:T(8,128)(2,1)S(1)} %all-to-all-done.kv_ref) | copy-start | bytes 3735556
  88.6 0.6 copy-start.5
  121.6 17.3 %all-to-all-start.3 = ((bf16[32,48,128]{2,1,0:T(8,128)(2,1)}), bf16[32,48,128]{2,1,0:T(8,128)(2,1)S(1)}, u32[]{:S(2)}, u32[]{:S(2)}) async-start(bf16[32,48,128]{2,1,0:T(8,128)(2,1)} %weight_part.1.after_ref), calls=%async_computation.3 | async-start | bytes 786432 | tf_op jit(solution)/shard_map/all_to_all | solution.py:292
  128.4 73.0 %reduce-scatter.2.cloned.1.call-start = ((), (), s32[]{:S(2)}) async-start(), calls=%async_computation.5 | async-start | bytes 368640 | tf_op jit(solution)/shard_map/reduce_scatter | solution.py:318
  138.9 12.2 %copy-start.4 = (bf16[32,48,128]{2,1,0:T(8,128)(2,1)}, bf16[32,48,128]{2,1,0:T(8,128)(2,1)S(1)}, u32[]{:S(2)}) copy-start(bf16[32,48,128]{2,1,0:T(8,128)(2,1)S(1)} %all-to-all-done.3.w_ref) | copy-start | bytes 1179652
  153.7 49.4 %all-to-all-start.1 = ((bf16[8,288,256]{2,1,0:T(8,128)(2,1)}), bf16[8,288,256]{2,1,0:T(8,128)(2,1)S(1)}, u32[]{:S(2)}, u32[]{:S(2)}) async-start(bf16[8,288,256]{2,1,0:T(8,128)(2,1)} %get-tuple-element.18), calls=%async_computation.1 | async-start | bytes 2359296 | tf_op jit(solution)/shard_map/all_to_all | solution.py:329
  203.1 1.1 copy-start.2
Sparse Core Ops, SparseCore 0:
  153.8 47.5 reduce-scatter.1

commit v4 on v3

--- a/solution.py
+++ b/solution.py
@@ -14,7 +14,7 @@
 SCALE = FACTOR * math.log2(math.e)
 BF = jnp.bfloat16
 F32 = jnp.float32
-VMEM = 60 * 1024 * 1024
+VMEM = 24 * 1024 * 1024
 LONG = pl.CostEstimate(flops=60_000_000_000, bytes_accessed=200_000_000, transcendentals=0)
 ANY = pl.BlockSpec(memory_space=pl.ANY)
 SCALAR = pl.BlockSpec(memory_space=pltpu.SMEM)
@@ -50,22 +50,25 @@
     return jnp.concatenate([x, jnp.where(row < 3, 1.0, 0.0)], axis=0)
 
 
-def pack_kernel(half_ref, k_ref, v_ref, q_ref, o_ref):
+def pack_heads(ref, o_ref):
+    turned = ref[...].astype(F32).T
+    for place in range(8):
+        a, b = heads_of(place)
+        o_ref[place, 0:144, :] = jnp.concatenate(
+            [turned[HD * a : HD * a + HD], turned[HD * b : HD * b + HD]], axis=0
+        ).astype(BF)
+
+
+def pack_keys_kernel(half_ref, k_ref, q_ref, o_ref):
+    pack_heads(k_ref, o_ref)
     every = q_ref[...].astype(F32)
     rows = jnp.where(half_ref[0] == 0, every[0:24], every[24:48])
-    for first, ref in ((0, k_ref), (144, v_ref)):
-        turned = ref[...].astype(F32).T
-        for place in range(8):
-            a, b = heads_of(place)
-            o_ref[place, first : first + 144, :] = jnp.concatenate(
-                [turned[HD * a : HD * a + HD], turned[HD * b : HD * b + HD]], axis=0
-            ).astype(BF)
     for place in range(8):
         a, b = heads_of(place)
         qa = rows[:, HD * a : HD * a + HD]
         qb = rows[:, HD * b : HD * b + HD]
         middle = jnp.concatenate([qa[16:24], qb[0:8]], axis=0)
-        o_ref[place, 288:304, :] = jnp.concatenate(
+        o_ref[place, 144:160, :] = jnp.concatenate(
             [qa[0:16], middle, qb[8:24], jnp.zeros((16, 40), F32)], axis=1
         ).astype(BF)
 
@@ -92,23 +95,32 @@
         weight = jnp.concatenate([total[:, 36 * k : 36 * k + 36] for k in range(3)], axis=0)
         for i in range(2):
             t = 2 * v + i
-            folded = [weight[HD * i + 8 * k : HD * i + 8 * k + 8] for k in range(9)]
-            folded = jnp.concatenate(folded + [jnp.zeros((8, 828), F32)], axis=1)
-            o_ref[t] = jnp.concatenate([rows[24 * t : 24 * t + 24], folded], axis=0).astype(BF)
+            folded = [weight[HD * i + 24 * k : HD * i + 24 * k + 24] for k in range(3)]
+            own = rows[24 * t : 24 * t + 24]
+            o_ref[t] = jnp.concatenate([own] + folded + [jnp.zeros((24, 20), F32)], axis=1).astype(BF)
 
 
 def finish_kernel(x_ref, q_ref, w_ref):
-    q_ref[...] = x_ref[0:24, :]
-    folded = x_ref[...].astype(F32)[24:32]
-    weight = jnp.concatenate([folded[:, 36 * k : 36 * k + 36] for k in range(9)], axis=0)
+    q_ref[...] = x_ref[:, 0:1152]
+    folded = x_ref[:, 1152:1280].astype(F32)
+    weight = jnp.concatenate([folded[:, 36 * k : 36 * k + 36] for k in range(3)], axis=0)
     w_ref[...] = weight.T
 
 
-def unpack_kernel(g_ref, after_ref, k_ref, v_ref):
+def unpack_kernel(g_ref, after_ref, k_ref, v_ref, held_ref, sems):
+    copies = []
+    for part in range(2):
+        copies.append(
+            pltpu.make_async_copy(
+                g_ref.at[:, pl.ds(144 * part, 144), :], held_ref.at[part], sems.at[part]
+            )
+        )
+        copies[part].start()
     for part, o_ref in ((0, k_ref), (1, v_ref)):
+        copies[part].wait()
         heads = [None] * 16
         for place in range(8):
-            block = g_ref[place, 144 * part : 144 * part + 144, :].astype(F32)
+            block = held_ref[part, place].astype(F32)
             a, b = heads_of(place)
             heads[a] = block[0:HD]
             heads[b] = block[HD : 2 * HD]
@@ -116,7 +128,19 @@
 
 
 def first_kernel(
-    half_ref, kv_ref, qg_ref, keep_ref, come_ref, st_ref, ot_ref, q_ref, ga_ref, qs_ref, qt_ref, kh_ref
+    half_ref,
+    k_ref,
+    v_ref,
+    qg_ref,
+    keep_ref,
+    come_ref,
+    st_ref,
+    ot_ref,
+    q_ref,
+    ga_ref,
+    qs_ref,
+    qt_ref,
+    s_ref,
 ):
     for block in range(32):
         piece = qg_ref[block].astype(F32)
@@ -138,31 +162,31 @@
 
     for h in range(2):
         q_ref[h] = qs_ref[h].astype(BF)
-        qt_ref[h, 0:72] = qs_ref[h].T.astype(BF)
-    st_ref[0:2, :] = jnp.full((2, ROWS), -1e30, F32)
-    st_ref[2:8, :] = jnp.zeros((6, ROWS), F32)
+        qt_ref[h] = qs_ref[h].T.astype(BF)
+
+    tops = [None, None]
+    for i in range(8):
+        keys = k_ref[i, 0:144, :].astype(F32)
+        for h in range(2):
+            s = nn(keys[HD * h : HD * h + HD].T.astype(BF), qt_ref[h])
+            s_ref[h, i] = s
+            top = jnp.max(s, axis=0, keepdims=True)
+            tops[h] = top if i == 0 else jnp.maximum(tops[h], top)
+
+    totals = [jnp.zeros((1, ROWS), F32)] * 2
+    weighted = [jnp.zeros((1, ROWS), F32)] * 2
     ot_ref[...] = jnp.zeros_like(ot_ref)
-
     for i in range(8):
-        keys = kv_ref[i, 0:144, :].astype(F32)
-        for h in range(2):
-            kh = with_ones(keys[HD * h : HD * h + HD]).T.astype(BF)
-            kh_ref[h, i] = kh
-            s = nn(kh[:, 0:72], qt_ref[h, 0:72])
-            st_ref[h : h + 1, :] = jnp.maximum(
-                st_ref[h : h + 1, :], jnp.max(s, axis=0, keepdims=True)
-            )
-    for h in range(2):
-        qt_ref[h, 72:80] = minus_parts(st_ref[h : h + 1, :])
-    for i in range(8):
-        values = kv_ref[i, 144:288, :].astype(F32)
+        values = v_ref[i].astype(F32)
         for h in range(2):
             vt = values[HD * h : HD * h + HD]
             u = nn(vt.T.astype(BF), ga_ref[h])
-            e = jnp.exp2(nn(kh_ref[h, i], qt_ref[h]) * SCALE)
-            st_ref[2 + h : 3 + h, :] += jnp.sum(e, axis=0, keepdims=True)
-            st_ref[4 + h : 5 + h, :] += jnp.sum(e * u, axis=0, keepdims=True)
+            e = jnp.exp2((s_ref[h, i] - tops[h]) * SCALE)
+            totals[h] = totals[h] + jnp.sum(e, axis=0, keepdims=True)
+            weighted[h] = weighted[h] + jnp.sum(e * u, axis=0, keepdims=True)
             ot_ref[h] += nn(vt.astype(BF), e.astype(BF))
+    rest = jnp.zeros((2, ROWS), F32)
+    st_ref[...] = jnp.concatenate(tops + totals + weighted + [rest], axis=0)
 
 
 def joined(sg_ref, h):
@@ -193,22 +217,21 @@
 
 
 def second_kernel(
-    kv_ref, q_ref, ga_ref, sg_ref, after_ref, grad_ref, dq_ref, qt_ref, gt_ref, gn_ref, dqt_ref
+    k_ref, v_ref, q_ref, ga_ref, sg_ref, after_ref, grad_ref, dq_ref, qt_ref, gt_ref, gn_ref, dqt_ref
 ):
     for h in range(2):
         highest, total, delta = joined(sg_ref, h)
         level = highest + jnp.log2(total) * (1.0 / SCALE)
         qt_ref[h, 0:72] = q_ref[h].astype(F32).T.astype(BF)
         qt_ref[h, 72:80] = minus_parts(level)
-        grads = ga_ref[h].astype(F32)
         gt_ref[h, 0:72] = ga_ref[h]
         gt_ref[h, 72:80] = minus_parts(delta)
-        gn_ref[h] = grads.T.astype(BF)
+        gn_ref[h] = ga_ref[h].astype(F32).T.astype(BF)
     dqt_ref[...] = jnp.zeros_like(dqt_ref)
 
     for i in range(8):
-        keys = kv_ref[i, 0:144, :].astype(F32)
-        values = kv_ref[i, 144:288, :].astype(F32)
+        keys = k_ref[i, 0:144, :].astype(F32)
+        values = v_ref[i].astype(F32)
         dks, dvs = [], []
         for h in range(2):
             kt = keys[HD * h : HD * h + HD]
@@ -242,30 +265,38 @@
     swap = [(0, 1), (1, 0)]
 
     place = jnp.full((1,), v, jnp.int32)
-    packed = pl.pallas_call(
-        pack_kernel,
-        out_shape=jax.ShapeDtypeStruct((8, 304, 256), BF),
-        in_specs=[SCALAR, HERE, HERE, HERE],
-        compiler_params=PARAMS,
-        name="pack_tokens",
-    )(place, key_rows, value_rows, query_rows)
-    tokens = lax.all_to_all(packed, CUBE, 0, 0, tiled=True)
+    packed_keys = pl.pallas_call(
+        pack_keys_kernel,
+        out_shape=jax.ShapeDtypeStruct((8, 160, 256), BF),
+        in_specs=[SCALAR, HERE, HERE],
+        compiler_params=PARAMS,
+        name="pack_keys",
+    )(place, key_rows, query_rows)
+    keys = lax.all_to_all(packed_keys, CUBE, 0, 0, tiled=True)
+    packed_values = pl.pallas_call(
+        pack_heads,
+        out_shape=jax.ShapeDtypeStruct((8, 144, 256), BF),
+        compiler_params=PARAMS,
+        name="pack_values",
+    )(value_rows)
 
     cotangent_half = lax.dynamic_slice_in_dim(cotangent, 384 * v, 384, 0)
     grad_half = lax.dot_general(
         out_weight, cotangent_half, (((1,), (1,)), ((), ())), preferred_element_type=F32
     ).astype(BF)
     grad_four = lax.all_gather(grad_half, "t")
+    packed_values, grad_four = lax.optimization_barrier((packed_values, grad_four))
+    values = lax.all_to_all(packed_values, CUBE, 0, 0, tiled=True)
     grad_keep = lax.dynamic_slice_in_dim(grad_four, 2 * v, 2, 0)
     grad_sent = lax.dynamic_slice_in_dim(grad_four, 2 - 2 * v, 2, 0)
     grad_come = lax.ppermute(grad_sent, "kv", swap)
 
-    query_pieces = lax.all_gather(tokens[:, 288:304, :].reshape(128, 256), "t")
+    query_pieces = lax.all_gather(keys[:, 144:160, :].reshape(128, 256), "t")
     query_pieces = query_pieces.reshape(32, 16, 256)
 
     stats, attn_turned, queries, grad_heads = pl.pallas_call(
         first_kernel,
-        in_specs=[SCALAR, HERE, HERE, HERE, HERE],
+        in_specs=[SCALAR] + [HERE] * 5,
         out_shape=[
             jax.ShapeDtypeStruct((8, ROWS), F32),
             jax.ShapeDtypeStruct((2, HD, ROWS), F32),
@@ -274,12 +305,12 @@
         ],
         scratch_shapes=[
             pltpu.VMEM((2, ROWS, HD), F32),
-            pltpu.VMEM((2, 80, ROWS), BF),
-            pltpu.VMEM((2, 8, 256, 80), BF),
+            pltpu.VMEM((2, HD, ROWS), BF),
+            pltpu.VMEM((2, 8, 256, ROWS), F32),
         ],
         compiler_params=PARAMS,
         name="first_pass",
-    )(place, tokens, query_pieces, grad_keep, grad_come)
+    )(place, keys, values, query_pieces, grad_keep, grad_come)
 
     gathered = lax.all_gather(stats, "t")
 
@@ -293,7 +324,7 @@
 
     grads, query_grad = pl.pallas_call(
         second_kernel,
-        in_specs=[HERE, HERE, HERE, HERE, ANY],
+        in_specs=[HERE] * 5 + [ANY],
         out_shape=[
             jax.ShapeDtypeStruct((8, 288, 256), BF),
             jax.ShapeDtypeStruct((8, 112, 128), BF),
@@ -306,17 +337,17 @@
         ],
         compiler_params=PARAMS,
         name="second_pass",
-    )(tokens, queries, grad_heads, gathered, weight_parts)
+    )(keys, values, queries, grad_heads, gathered, weight_parts)
 
     query_come = lax.all_to_all(query_grad, CUBE, 0, 0, tiled=True)
     scattered = pl.pallas_call(
         scatter_kernel,
-        out_shape=jax.ShapeDtypeStruct((4, 32, 1152), BF),
+        out_shape=jax.ShapeDtypeStruct((4, 24, 1280), BF),
         compiler_params=PARAMS,
         name="scatter_pack",
     )(query_come, weight_come)
     summed = lax.psum_scatter(
-        scattered.reshape(128, 1152), "t", scatter_dimension=0, tiled=True
+        scattered.reshape(96, 1280), "t", scatter_dimension=0, tiled=True
     )
     query_out, weight_out = pl.pallas_call(
         finish_kernel,
@@ -330,7 +361,8 @@
     key_out, value_out = pl.pallas_call(
         unpack_kernel,
         out_shape=[jax.ShapeDtypeStruct((256, 1152), BF)] * 2,
-        in_specs=[HERE, ANY],
+        in_specs=[pl.BlockSpec(memory_space=pltpu.HBM), ANY],
+        scratch_shapes=[pltpu.VMEM((2, 8, 144, 256), BF), pltpu.SemaphoreType.DMA((2,))],
         compiler_params=PARAMS,
         name="unpack_grads",
     )(grads_back, weight_out)

time: 214 us -> 207 us (0.967)
  Pallas kernels: 33.6 us -> 20.7 us
  blocking collectives: 96.7 us -> 86.9 us
  local copies, waits for them, and re-layouts: 2.39 us -> 12.1 us
  starting transfers between devices: 24.1 us -> 29.9 us
    all_gather x1, blocking collectives: 47.1 us -> 32.1 us  [on_device(): grad_four = lax.all_gather(grad_half, 't')]
    unnamed x12 -> x34, local copies, waits for them, and re-layouts: 1.72 us -> 12 us
    pallas_call x4 -> x5, Pallas kernels: 26.3 us -> 17.8 us  [the longest x1 7.93 us: on_device(): pl.pallas_call(second_kernel, in_specs=[HERE] * 5 + [ANY], out_shape=[jax...]
    all_gather x1, blocking collectives: 18.9 us -> 25.6 us  [on_device(): query_pieces = lax.all_gather(keys[:, 144:160, :].reshape(128, 256), 't')]
    all_to_all x1 -> x2, starting transfers between devices: 8.65 us -> 13.6 us  [the longest x1 8.49 us: on_device(): keys = lax.all_to_all(packed_keys, CUBE, 0, 0, tiled=True)]
    pallas_call x1, Pallas kernels: 3.17 us -> 0.72 us  [on_device(): pl.pallas_call(weight_kernel, out_shape=jax.ShapeDtypeStruct((32, 48, 128...]
  transfers between devices with their start and end apart: 5 -> 6, of which waited for: 1 -> 1; matrix products, arithmetic and copies ran while one was open for 1% -> 0% of each run, Pallas kernels for 6% -> 4%
where the time goes in v4:
time: 207 us; the launch traced here: 206 us
  blocking collectives  86.9 us (42%)
  waiting for transfers between devices  41.9 us (20%)
  starting transfers between devices  29.9 us (14%)
  Pallas kernels  20.7 us (10%)
  between operations  14.2 us (7%)
  local copies, waits for them, and re-layouts  12.1 us (6%)
    reduce_scatter x1, waiting for transfers between devices, on_device(): lax.psum_scatter(scattered.reshape(96, 1280), 't', scatter_dimension=0, t...  41.9 us
    all_gather x1, blocking collectives, on_device(): grad_four = lax.all_gather(grad_half, 't')  32.1 us
    all_gather x1, blocking collectives, on_device(): query_pieces = lax.all_gather(keys[:, 144:160, :].reshape(128, 256), 't')  25.6 us
    all_gather x1, blocking collectives, on_device(): gathered = lax.all_gather(stats, 't')  17.3 us
    unnamed x34, local copies, waits for them, and re-layouts  12 us
    all_to_all x1, blocking collectives, on_device(): query_come = lax.all_to_all(query_grad, CUBE, 0, 0, tiled=True)  11.9 us
    all_to_all x1, starting transfers between devices, on_device(): keys = lax.all_to_all(packed_keys, CUBE, 0, 0, tiled=True)  8.49 us
    pallas_call x1, Pallas kernels, on_device(): pl.pallas_call(second_kernel, in_specs=[HERE] * 5 + [ANY], out_shape=[jax...  7.93 us
  transfers between devices with their start and end apart: 6, of which 1 were waited for; matrix products, arithmetic and copies ran while one was open for 0% of the time, Pallas kernels for 4%

profile of v4, /device:TPU:64, one launch (start us, length us, event | category | flops | bytes accessed | tf_op | source)
XLA Modules:
  0.0 206.1 jit_solution(2957183265587308616)
XLA Ops:
  7.2 0.0 copy-start
  7.2 0.0 copy-start.6
  7.2 1.1 copy-done.6
  8.3 0.9 copy-done.12
  9.2 1.2 pack_keys.1
  10.4 8.5 %all-to-all-start = ((bf16[8,160,256]{2,1,0:T(8,128)(2,1)}), bf16[8,160,256]{2,1,0:T(8,128)(2,1)S(1)}, u32[]{:S(2)}, u32[]{:S(2)}) async-start(bf16[8,160,256]{2,1,0:T(8,128)(2,1)} %pack_keys.1), calls=%async_computation | async-start | bytes 1310720 | tf_op jit(solution)/shard_map/all_to_all | solution.py:275
  18.9 0.0 copy-done.7
  18.9 0.2 pack_values.1
  19.1 0.0 copy-start.4
  19.1 0.8 copy-done.4
  19.9 0.0 copy-done
  19.9 0.4 fusion
  20.4 32.1 %all-gather = bf16[288,384]{1,0:T(8,128)(2,1)S(1)} all-gather(bf16[72,384]{1,0:T(8,128)(2,1)S(1)} %fusion), channel_id=2, replica_groups=mesh['y'=4,'xh'=2,'core'=2,'t'=4,'j'=4,'kv'=2] {'t'}, dimensions={0}, use_global_device_ids=true | all-gather | bytes 276480 | tf_op jit(solution)/shard_map/all_gather | solution.py:287
  52.5 0.0 all-to-all-done.k_ref
  52.5 5.1 %all-to-all-start.1 = ((bf16[8,144,256]{2,1,0:T(8,128)(2,1)}), bf16[8,144,256]{2,1,0:T(8,128)(2,1)S(1)}, u32[]{:S(2)}, u32[]{:S(2)}) async-start(bf16[8,144,256]{2,1,0:T(8,128)(2,1)} %copy-done.4), calls=%async_computation.1 | async-start | bytes 1179648 | tf_op jit(solution)/shard_map/all_to_all | solution.py:289
  57.6 3.4 %collective-permute-start = (bf16[2,72,384]{2,1,0:T(8,128)(2,1)S(1)}, bf16[2,72,384]{2,1,0:T(8,128)(2,1)S(1)}, u32[]{:S(2)}, u32[]{:S(2)}) collective-permute-start(bf16[2,72,384]{2,1,0:T(8,128)(2,1)S(1)} %get-tuple-element.28), channel_id=1, source_target_pairs={{0,1},{1,0},{2,3},{3,2},{4,5},{5,4},{6,7},{7,6},{8,9},{9,8},{10,11... | collective-permute-start | bytes 331784 | tf_op jit(solution)/shard_map/ppermute | solution.py:292
  61.0 25.6 %all_gather.17 = bf16[4,128,256]{2,1,0:T(8,128)(2,1)S(1)} all-gather(bf16[1,128,256]{2,1,0:T(8,128)(2,1)S(1)} %bitcast.29), channel_id=1, replica_groups=mesh['y'=4,'xh'=2,'core'=2,'t'=4,'j'=4,'kv'=2] {'t'}, dimensions={0}, use_global_device_ids=true | all-gather | bytes 327680 | tf_op jit(solution)/shard_map/all_gather | solution.py:294
  86.6 0.0 collective-permute-done.come_ref
  86.6 0.6 copy-done.13
  87.2 0.0 all-to-all-done.1.v_ref
  87.2 0.9 copy-done.14
  88.1 6.2 %first_pass.1 = (f32[8,768]{1,0:T(8,128)S(1)}, f32[2,72,768]{2,1,0:T(8,128)S(1)}, bf16[2,768,72]{2,1,0:T(8,128)(2,1)S(1)}, bf16[2,72,768]{2,1,0:T(8,128)(2,1)S(1)}) custom-call(s32[1]{0:T(128)} %bitcast.half_ref, bf16[8,160,256]{2,1,0:T(8,128)(2,1)S(1)} %all-to-all-done.k_ref, bf16[8,144,256]{2,1,0:T(8,128)(2,1)S(1)} %all-to-all-done.1.v_ref, ...), custom_call_target="tpu_custom_call" | custom-call | tf_op jit(solution)/shard_map/first_pass/pallas_call | solution.py:297
  94.3 0.0 copy-start.8
  94.3 0.7 copy-done.8
  95.0 0.7 copy-done.10
  95.7 17.3 %all-gather.1 = f32[32,768]{1,0:T(8,128)S(1)} all-gather(f32[8,768]{1,0:T(8,128)S(1)} %get-tuple-element.20.st_ref), channel_id=3, replica_groups=mesh['y'=4,'xh'=2,'core'=2,'t'=4,'j'=4,'kv'=2] {'t'}, dimensions={0}, use_global_device_ids=true | all-gather | bytes 122880 | tf_op jit(solution)/shard_map/all_gather | solution.py:315
  113.0 0.7 weight_part.1.after_ref
  113.8 0.0 copy-start.2
  113.8 0.7 copy-done.2
  114.5 7.2 %all-to-all-start.4 = ((bf16[32,48,128]{2,1,0:T(8,128)(2,1)}), bf16[32,48,128]{2,1,0:T(8,128)(2,1)}, u32[]{:S(2)}, u32[]{:S(2)}) async-start(bf16[32,48,128]{2,1,0:T(8,128)(2,1)} %copy-done.2), calls=%async_computation.4 | async-start | bytes 786432 | tf_op jit(solution)/shard_map/all_to_all | solution.py:323
  121.7 0.2 reduce-scatter.2.cloned.1.call-start
  122.0 0.0 copy-start.3
  122.0 1.0 copy-done.3
  123.0 1.0 copy-done.9
  124.0 0.9 copy-done.11
  124.9 7.9 %second_pass.1 = (bf16[8,288,256]{2,1,0:T(8,128)(2,1)S(1)}, bf16[8,112,128]{2,1,0:T(8,128)(2,1)S(1)}) custom-call(bf16[8,160,256]{2,1,0:T(8,128)(2,1)S(1)} %all-to-all-done.k_ref, bf16[8,144,256]{2,1,0:T(8,128)(2,1)S(1)} %all-to-all-done.1.v_ref, bf16[2,768,72]{2,1,0:T(8,128)(2,1)S(1)} %copy-done.9, bf16[2,72,768]{2,1,0:T(8,128)(2,1)S(1)} %copy-done.11, ...), custom_call_target="tpu_custom_call" | custom-call | tf_op jit(solution)/shard_map/second_pass/pallas_call | solution.py:325
  132.8 1.0 copy-done.5
  133.8 0.0 all-to-all-done.4.w_ref
  133.8 11.9 %all_to_all.25.g_ref = bf16[8,112,128]{2,1,0:T(8,128)(2,1)S(1)} all-to-all(bf16[8,112,128]{2,1,0:T(8,128)(2,1)S(1)} %get-tuple-element.23), channel_id=1, replica_groups=mesh['y'=4,'xh'=2,'core'=2,'t'=4,'j'=4,'kv'=2] {'j','kv'}, dimensions={0} | all-to-all | bytes 458752 | tf_op jit(solution)/shard_map/all_to_all | solution.py:342
  145.7 2.3 %scatter_pack.1 = bf16[4,24,1280]{2,1,0:T(8,128)(2,1)} custom-call(bf16[8,112,128]{2,1,0:T(8,128)(2,1)S(1)} %all_to_all.25.g_ref, bf16[32,48,128]{2,1,0:T(8,128)(2,1)} %all-to-all-done.4.w_ref), custom_call_target="tpu_custom_call" | custom-call | tf_op jit(solution)/shard_map/scatter_pack/pallas_call | solution.py:343
  148.1 0.0 reduce-scatter.2.cloned.1.call-update
  148.1 5.5 %all-to-all-start.2 = ((bf16[8,288,256]{2,1,0:T(8,128)(2,1)}), bf16[8,288,256]{2,1,0:T(8,128)(2,1)S(1)}, u32[]{:S(2)}, u32[]{:S(2)}) async-start(bf16[8,288,256]{2,1,0:T(8,128)(2,1)} %copy-done.5), calls=%async_computation.2 | async-start | bytes 2359296 | tf_op jit(solution)/shard_map/all_to_all | solution.py:360
  153.6 41.9 %reduce-scatter.2.cloned.1.call-done.x_ref = bf16[24,1280]{1,0:T(8,128)(2,1)} async-done(((bf16[96,1280]{1,0:T(8,128)(2,1)}), bf16[24,1280]{1,0:T(8,128)(2,1)}) %reduce-scatter.2.cloned.1.call-update) | async-done | bytes 61456 | tf_op jit(solution)/shard_map/reduce_scatter | solution.py:349
  195.5 0.8 copy-done.16
  196.3 0.7 finish.1
  197.1 0.0 all-to-all-done.2.g_ref
  197.1 0.7 copy-done.15
  197.8 1.4 unpack_grads.1
  (14 shorter events, 0.1 us)
Async XLA Ops:
  7.2 12.7 %copy-start = (bf16[72,1152]{1,0:T(8,128)(2,1)S(1)}, bf16[72,1152]{1,0:T(8,128)(2,1)}, u32[]{:S(2)}) copy-start(bf16[72,1152]{1,0:T(8,128)(2,1)} %param.9) | copy-start | bytes 497668
  7.2 1.1 copy-start.6
  8.3 0.9 copy-start.12
  9.2 9.7 %copy-start.7 = (bf16[1,256,1152]{2,1,0:T(8,128)(2,1)S(1)}, bf16[1,256,1152]{2,1,0:T(8,128)(2,1)}, u32[]{:S(2)}) copy-start(bf16[1,256,1152]{2,1,0:T(8,128)(2,1)} %param.7) | copy-start | bytes 1769476
  9.2 10.7 %copy-start.1 = (bf16[1,768,1152]{2,1,0:T(8,128)(2,1)S(1)}, bf16[1,768,1152]{2,1,0:T(8,128)(2,1)}, u32[]{:S(2)}) copy-start(bf16[1,768,1152]{2,1,0:T(8,128)(2,1)} %param.8) | copy-start | bytes 5308420
  10.4 42.1 %all-to-all-start = ((bf16[8,160,256]{2,1,0:T(8,128)(2,1)}), bf16[8,160,256]{2,1,0:T(8,128)(2,1)S(1)}, u32[]{:S(2)}, u32[]{:S(2)}) async-start(bf16[8,160,256]{2,1,0:T(8,128)(2,1)} %pack_keys.1), calls=%async_computation | async-start | bytes 1310720 | tf_op jit(solution)/shard_map/all_to_all | solution.py:275
  19.1 0.8 copy-start.4
  52.5 34.7 %all-to-all-start.1 = ((bf16[8,144,256]{2,1,0:T(8,128)(2,1)}), bf16[8,144,256]{2,1,0:T(8,128)(2,1)S(1)}, u32[]{:S(2)}, u32[]{:S(2)}) async-start(bf16[8,144,256]{2,1,0:T(8,128)(2,1)} %copy-done.4), calls=%async_computation.1 | async-start | bytes 1179648 | tf_op jit(solution)/shard_map/all_to_all | solution.py:289
  57.6 28.9 %collective-permute-start = (bf16[2,72,384]{2,1,0:T(8,128)(2,1)S(1)}, bf16[2,72,384]{2,1,0:T(8,128)(2,1)S(1)}, u32[]{:S(2)}, u32[]{:S(2)}) collective-permute-start(bf16[2,72,384]{2,1,0:T(8,128)(2,1)S(1)} %get-tuple-element.28), channel_id=1, source_target_pairs={{0,1},{1,0},{2,3},{3,2},{4,5},{5,4},{6,7},{7,6},{8,9},{9,8},{10,11... | collective-permute-start | bytes 331784 | tf_op jit(solution)/shard_map/ppermute | solution.py:292
  86.6 0.6 copy-start.13
  87.2 0.9 copy-start.14
  94.3 0.7 copy-start.8
  95.0 0.7 copy-start.10
  113.8 0.7 copy-start.2
  114.5 19.3 %all-to-all-start.4 = ((bf16[32,48,128]{2,1,0:T(8,128)(2,1)}), bf16[32,48,128]{2,1,0:T(8,128)(2,1)}, u32[]{:S(2)}, u32[]{:S(2)}) async-start(bf16[32,48,128]{2,1,0:T(8,128)(2,1)} %copy-done.2), calls=%async_computation.4 | async-start | bytes 786432 | tf_op jit(solution)/shard_map/all_to_all | solution.py:323
  121.7 73.8 %reduce-scatter.2.cloned.1.call-start = ((), (), s32[]{:S(2)}) async-start(), calls=%async_computation.6 | async-start | bytes 307200 | tf_op jit(solution)/shard_map/reduce_scatter | solution.py:349
  122.0 1.0 copy-start.3
  123.0 1.0 copy-start.9
  124.0 0.9 copy-start.11
  132.8 1.0 copy-start.5
  148.1 49.0 %all-to-all-start.2 = ((bf16[8,288,256]{2,1,0:T(8,128)(2,1)}), bf16[8,288,256]{2,1,0:T(8,128)(2,1)S(1)}, u32[]{:S(2)}, u32[]{:S(2)}) async-start(bf16[8,288,256]{2,1,0:T(8,128)(2,1)} %copy-done.5), calls=%async_computation.2 | async-start | bytes 2359296 | tf_op jit(solution)/shard_map/all_to_all | solution.py:360
  195.5 0.8 copy-start.16
  197.1 0.7 copy-start.15
Sparse Core Ops, SparseCore 0:
  148.2 47.2 reduce-scatter.1

commit v5 on v4

--- a/solution.py
+++ b/solution.py
@@ -107,7 +107,7 @@
     w_ref[...] = weight.T
 
 
-def unpack_kernel(g_ref, after_ref, k_ref, v_ref, held_ref, sems):
+def unpack_kernel(g_ref, k_ref, v_ref, held_ref, sems):
     copies = []
     for part in range(2):
         copies.append(
@@ -127,21 +127,7 @@
         o_ref[...] = jnp.concatenate(heads, axis=0).T.astype(BF)
 
 
-def first_kernel(
-    half_ref,
-    k_ref,
-    v_ref,
-    qg_ref,
-    keep_ref,
-    come_ref,
-    st_ref,
-    ot_ref,
-    q_ref,
-    ga_ref,
-    qs_ref,
-    qt_ref,
-    s_ref,
-):
+def rows_of(qg_ref, qs_ref):
     for block in range(32):
         piece = qg_ref[block].astype(F32)
         base = 24 * block
@@ -150,18 +136,10 @@
         qs_ref[1, base : base + 8, :] = piece[8:16, 72:144]
         qs_ref[1, base + 8 : base + 24, :] = piece[:, 144:216]
 
-    @pl.when(half_ref[0] == 0)
-    def _():
-        ga_ref[:, :, 0:384] = keep_ref[...]
-        ga_ref[:, :, 384:768] = come_ref[...]
-
-    @pl.when(half_ref[0] == 1)
-    def _():
-        ga_ref[:, :, 0:384] = come_ref[...]
-        ga_ref[:, :, 384:768] = keep_ref[...]
-
+
+def first_kernel(k_ref, v_ref, qg_ref, ga_ref, st_ref, ot_ref, qs_ref, qt_ref, s_ref):
+    rows_of(qg_ref, qs_ref)
     for h in range(2):
-        q_ref[h] = qs_ref[h].astype(BF)
         qt_ref[h] = qs_ref[h].T.astype(BF)
 
     tops = [None, None]
@@ -217,12 +195,14 @@
 
 
 def second_kernel(
-    k_ref, v_ref, q_ref, ga_ref, sg_ref, after_ref, grad_ref, dq_ref, qt_ref, gt_ref, gn_ref, dqt_ref
+    k_ref, v_ref, qg_ref, ga_ref, sg_ref, grad_ref, dq_ref, qs_ref, q_ref, qt_ref, gt_ref, gn_ref, dqt_ref
 ):
+    rows_of(qg_ref, qs_ref)
     for h in range(2):
         highest, total, delta = joined(sg_ref, h)
         level = highest + jnp.log2(total) * (1.0 / SCALE)
-        qt_ref[h, 0:72] = q_ref[h].astype(F32).T.astype(BF)
+        q_ref[h] = qs_ref[h].astype(BF)
+        qt_ref[h, 0:72] = qs_ref[h].T.astype(BF)
         qt_ref[h, 72:80] = minus_parts(level)
         gt_ref[h, 0:72] = ga_ref[h]
         gt_ref[h, 72:80] = minus_parts(delta)
@@ -269,7 +249,7 @@
         pack_keys_kernel,
         out_shape=jax.ShapeDtypeStruct((8, 160, 256), BF),
         in_specs=[SCALAR, HERE, HERE],
-        compiler_params=PARAMS,
+        compiler_params=pltpu.CompilerParams(vmem_limit_bytes=60 * 1024 * 1024),
         name="pack_keys",
     )(place, key_rows, query_rows)
     keys = lax.all_to_all(packed_keys, CUBE, 0, 0, tiled=True)
@@ -294,14 +274,16 @@
     query_pieces = lax.all_gather(keys[:, 144:160, :].reshape(128, 256), "t")
     query_pieces = query_pieces.reshape(32, 16, 256)
 
-    stats, attn_turned, queries, grad_heads = pl.pallas_call(
+    grad_heads = jnp.where(
+        v == 0,
+        jnp.concatenate([grad_keep, grad_come], axis=2),
+        jnp.concatenate([grad_come, grad_keep], axis=2),
+    )
+    stats, attn_turned = pl.pallas_call(
         first_kernel,
-        in_specs=[SCALAR] + [HERE] * 5,
         out_shape=[
             jax.ShapeDtypeStruct((8, ROWS), F32),
             jax.ShapeDtypeStruct((2, HD, ROWS), F32),
-            jax.ShapeDtypeStruct((2, ROWS, HD), BF),
-            jax.ShapeDtypeStruct((2, HD, ROWS), BF),
         ],
         scratch_shapes=[
             pltpu.VMEM((2, ROWS, HD), F32),
@@ -310,7 +292,7 @@
         ],
         compiler_params=PARAMS,
         name="first_pass",
-    )(place, keys, values, query_pieces, grad_keep, grad_come)
+    )(keys, values, query_pieces, grad_heads)
 
     gathered = lax.all_gather(stats, "t")
 
@@ -322,14 +304,16 @@
     )(gathered, stats, attn_turned, cotangent)
     weight_come = lax.all_to_all(weight_parts, DP + ("kv",), 0, 0, tiled=True)
 
+    gathered, weight_parts = lax.optimization_barrier((gathered, weight_parts))
     grads, query_grad = pl.pallas_call(
         second_kernel,
-        in_specs=[HERE] * 5 + [ANY],
         out_shape=[
             jax.ShapeDtypeStruct((8, 288, 256), BF),
             jax.ShapeDtypeStruct((8, 112, 128), BF),
         ],
         scratch_shapes=[
+            pltpu.VMEM((2, ROWS, HD), F32),
+            pltpu.VMEM((2, ROWS, HD), BF),
             pltpu.VMEM((2, 80, ROWS), BF),
             pltpu.VMEM((2, 80, ROWS), BF),
             pltpu.VMEM((2, ROWS, HD), BF),
@@ -337,7 +321,7 @@
         ],
         compiler_params=PARAMS,
         name="second_pass",
-    )(keys, values, queries, grad_heads, gathered, weight_parts)
+    )(keys, values, query_pieces, grad_heads, gathered)
 
     query_come = lax.all_to_all(query_grad, CUBE, 0, 0, tiled=True)
     scattered = pl.pallas_call(
@@ -361,11 +345,11 @@
     key_out, value_out = pl.pallas_call(
         unpack_kernel,
         out_shape=[jax.ShapeDtypeStruct((256, 1152), BF)] * 2,
-        in_specs=[pl.BlockSpec(memory_space=pltpu.HBM), ANY],
+        in_specs=[pl.BlockSpec(memory_space=pl.ANY)],
         scratch_shapes=[pltpu.VMEM((2, 8, 144, 256), BF), pltpu.SemaphoreType.DMA((2,))],
         compiler_params=PARAMS,
         name="unpack_grads",
-    )(grads_back, weight_out)
+    )(grads_back)
     return (key_out[None], value_out[None], query_out[None], weight_out.T)
 
 

time: 207 us -> 203 us (0.981)
  local copies, waits for them, and re-layouts: 12.1 us -> 5.96 us
  waiting for transfers between devices: 41.9 us -> 46.6 us
  blocking collectives: 86.9 us -> 82.4 us
    unnamed x34 -> x18, local copies, waits for them, and re-layouts: 12 us -> 5.29 us
    all_gather x1, blocking collectives: 25.6 us -> 19.8 us  [on_device(): query_pieces = lax.all_gather(keys[:, 144:160, :].reshape(128, 256), 't')]
    ppermute x1, waiting for transfers between devices: 0.01 us -> 4.64 us  [on_device(): grad_come = lax.ppermute(grad_sent, 'kv', swap)]
  transfers between devices with their start and end apart: 6 -> 6, of which waited for: 1 -> 3; matrix products, arithmetic and copies ran while one was open for 0% -> 1% of each run, Pallas kernels for 4% -> 4%
where the time goes in v5:
time: 203 us; the launch traced here: 202 us
  blocking collectives  82.4 us (41%)
  waiting for transfers between devices  46.6 us (23%)
  starting transfers between devices  29.7 us (15%)
  Pallas kernels  22 us (11%)
  between operations  14.2 us (7%)
  local copies, waits for them, and re-layouts  5.96 us (3%)
    reduce_scatter x1, waiting for transfers between devices, on_device(): lax.psum_scatter(scattered.reshape(96, 1280), 't', scatter_dimension=0, t...  41.6 us
    all_gather x1, blocking collectives, on_device(): grad_four = lax.all_gather(grad_half, 't')  32.1 us
    all_gather x1, blocking collectives, on_device(): query_pieces = lax.all_gather(keys[:, 144:160, :].reshape(128, 256), 't')  19.8 us
    all_gather x1, blocking collectives, on_device(): gathered = lax.all_gather(stats, 't')  17.4 us
    all_to_all x1, blocking collectives, on_device(): query_come = lax.all_to_all(query_grad, CUBE, 0, 0, tiled=True)  13.1 us
    all_to_all x1, starting transfers between devices, on_device(): keys = lax.all_to_all(packed_keys, CUBE, 0, 0, tiled=True)  8.49 us
    pallas_call x1, Pallas kernels, on_device(): pl.pallas_call(second_kernel, out_shape=[jax.ShapeDtypeStruct((8, 288, 25...  7.94 us
    all_to_all x1, starting transfers between devices, on_device(): weight_come = lax.all_to_all(weight_parts, DP + ('kv',), 0, 0, tiled=True)  6.95 us
  transfers between devices with their start and end apart: 6, of which 3 were waited for; matrix products, arithmetic and copies ran while one was open for 1% of the time, Pallas kernels for 4%

profile of v5, /device:TPU:64, one launch (start us, length us, event | category | flops | bytes accessed | tf_op | source)
XLA Modules:
  0.0 201.9 jit_solution(5642388545683794242)
XLA Ops:
  7.2 0.0 copy-start
  7.2 0.0 copy-start.7
  7.2 0.0 copy-start.1
  7.2 2.4 %pack_keys.1 = bf16[8,160,256]{2,1,0:T(8,128)(2,1)} custom-call(s32[1]{0:T(128)} %bitcast.half_ref, bf16[256,1152]{1,0:T(8,128)(2,1)} %bitcast.27, bf16[48,1152]{1,0:T(8,128)(2,1)} %bitcast.29), custom_call_target="tpu_custom_call" | custom-call | tf_op jit(solution)/shard_map/pack_keys/pallas_call | solution.py:248
  9.6 8.5 %all-to-all-start = ((bf16[8,160,256]{2,1,0:T(8,128)(2,1)}), bf16[8,160,256]{2,1,0:T(8,128)(2,1)S(1)}, u32[]{:S(2)}, u32[]{:S(2)}) async-start(bf16[8,160,256]{2,1,0:T(8,128)(2,1)} %pack_keys.1), calls=%async_computation | async-start | bytes 1310720 | tf_op jit(solution)/shard_map/all_to_all | solution.py:255
  18.1 0.0 copy-done.7
  18.1 0.2 pack_values.1
  18.4 0.0 copy-start.2
  18.4 0.8 copy-done.2
  19.2 0.0 copy-done
  19.2 0.0 copy-done.1
  19.2 0.4 fusion
  19.6 32.1 %all-gather = bf16[288,384]{1,0:T(8,128)(2,1)S(1)} all-gather(bf16[72,384]{1,0:T(8,128)(2,1)S(1)} %fusion), channel_id=2, replica_groups=mesh['y'=4,'xh'=2,'core'=2,'t'=4,'j'=4,'kv'=2] {'t'}, dimensions={0}, use_global_device_ids=true | all-gather | bytes 276480 | tf_op jit(solution)/shard_map/all_gather | solution.py:267
  51.8 0.0 all-to-all-done.k_ref
  51.8 5.1 %all-to-all-start.1 = ((bf16[8,144,256]{2,1,0:T(8,128)(2,1)}), bf16[8,144,256]{2,1,0:T(8,128)(2,1)S(1)}, u32[]{:S(2)}, u32[]{:S(2)}) async-start(bf16[8,144,256]{2,1,0:T(8,128)(2,1)} %copy-done.2), calls=%async_computation.1 | async-start | bytes 1179648 | tf_op jit(solution)/shard_map/all_to_all | solution.py:269
  56.9 0.7 constant_dynamic-slice_fusion.1
  57.5 3.4 %collective-permute-start = (bf16[2,72,384]{2,1,0:T(8,128)(2,1)}, bf16[2,72,384]{2,1,0:T(8,128)(2,1)S(1)}, u32[]{:S(2)}, u32[]{:S(2)}) collective-permute-start(bf16[2,72,384]{2,1,0:T(8,128)(2,1)} %get-tuple-element.27), channel_id=1, source_target_pairs={{0,1},{1,0},{2,3},{3,2},{4,5},{5,4},{6,7},{7,6},{8,9},{9,8},{10,11... | collective-permute-start | bytes 331784 | tf_op jit(solution)/shard_map/ppermute | solution.py:272
  60.9 4.6 %collective-permute-done = bf16[2,72,384]{2,1,0:T(8,128)(2,1)S(1)} collective-permute-done((bf16[2,72,384]{2,1,0:T(8,128)(2,1)}, bf16[2,72,384]{2,1,0:T(8,128)(2,1)S(1)}, u32[]{:S(2)}, u32[]{:S(2)}) %collective-permute-start) | collective-permute-done | bytes 110624 | tf_op jit(solution)/shard_map/ppermute | solution.py:272
  65.5 0.7 maximum_select_fusion.ga_ref
  66.3 19.8 %all_gather.17 = bf16[4,128,256]{2,1,0:T(8,128)(2,1)S(1)} all-gather(bf16[1,128,256]{2,1,0:T(8,128)(2,1)S(1)} %bitcast.28), channel_id=1, replica_groups=mesh['y'=4,'xh'=2,'core'=2,'t'=4,'j'=4,'kv'=2] {'t'}, dimensions={0}, use_global_device_ids=true | all-gather | bytes 327680 | tf_op jit(solution)/shard_map/all_gather | solution.py:274
  86.1 0.0 all-to-all-done.1.v_ref
  86.1 0.0 copy-start.3
  86.1 0.9 copy-done.3
  87.1 6.1 %first_pass.1 = (f32[8,768]{1,0:T(8,128)S(1)}, f32[2,72,768]{2,1,0:T(8,128)S(1)}) custom-call(bf16[8,160,256]{2,1,0:T(8,128)(2,1)S(1)} %all-to-all-done.k_ref, bf16[8,144,256]{2,1,0:T(8,128)(2,1)S(1)} %all-to-all-done.1.v_ref, bf16[32,16,256]{2,1,0:T(8,128)(2,1)S(1)} %bitcast.21, bf16[2,72,768]{2,1,0:T(8,128)(2,1)S(1)} %copy-done.3), custom_call_target="tpu_custom_call" | custom-call | tf_op jit(solution)/shard_map/first_pass/pallas_call | solution.py:282
  93.2 17.4 %all-gather.1 = f32[32,768]{1,0:T(8,128)S(1)} all-gather(f32[8,768]{1,0:T(8,128)S(1)} %get-tuple-element.17.st_ref), channel_id=3, replica_groups=mesh['y'=4,'xh'=2,'core'=2,'t'=4,'j'=4,'kv'=2] {'t'}, dimensions={0}, use_global_device_ids=true | all-gather | bytes 122880 | tf_op jit(solution)/shard_map/all_gather | solution.py:297
  110.6 0.7 weight_part.1
  111.3 0.0 copy-start.5
  111.3 0.7 copy-done.5
  112.1 7.0 %all-to-all-start.4 = ((bf16[32,48,128]{2,1,0:T(8,128)(2,1)}), bf16[32,48,128]{2,1,0:T(8,128)(2,1)}, u32[]{:S(2)}, u32[]{:S(2)}) async-start(bf16[32,48,128]{2,1,0:T(8,128)(2,1)} %copy-done.5), calls=%async_computation.4 | async-start | bytes 786432 | tf_op jit(solution)/shard_map/all_to_all | solution.py:305
  119.0 0.2 reduce-scatter.2.cloned.1.call-start
  119.2 0.0 copy-start.4
  119.3 0.9 copy-done.4
  120.2 7.9 %second_pass.1 = (bf16[8,288,256]{2,1,0:T(8,128)(2,1)S(1)}, bf16[8,112,128]{2,1,0:T(8,128)(2,1)S(1)}) custom-call(bf16[8,160,256]{2,1,0:T(8,128)(2,1)S(1)} %all-to-all-done.k_ref, bf16[8,144,256]{2,1,0:T(8,128)(2,1)S(1)} %all-to-all-done.1.v_ref, bf16[32,16,256]{2,1,0:T(8,128)(2,1)S(1)} %bitcast.22, bf16[2,72,768]{2,1,0:T(8,128)(2,1)S(1)} %copy-done.4, ...), custom_call_target="tpu_custom_call" | custom-call | tf_op jit(solution)/shard_map/second_pass/pallas_call | solution.py:308
  128.1 0.0 copy-start.6
  128.1 1.0 copy-done.6
  129.2 0.3 all-to-all-done.4.w_ref
  129.4 13.1 %all_to_all.25.g_ref = bf16[8,112,128]{2,1,0:T(8,128)(2,1)S(1)} all-to-all(bf16[8,112,128]{2,1,0:T(8,128)(2,1)S(1)} %get-tuple-element.23), channel_id=1, replica_groups=mesh['y'=4,'xh'=2,'core'=2,'t'=4,'j'=4,'kv'=2] {'j','kv'}, dimensions={0} | all-to-all | bytes 458752 | tf_op jit(solution)/shard_map/all_to_all | solution.py:326
  142.5 2.3 %scatter_pack.1 = bf16[4,24,1280]{2,1,0:T(8,128)(2,1)} custom-call(bf16[8,112,128]{2,1,0:T(8,128)(2,1)S(1)} %all_to_all.25.g_ref, bf16[32,48,128]{2,1,0:T(8,128)(2,1)} %all-to-all-done.4.w_ref), custom_call_target="tpu_custom_call" | custom-call | tf_op jit(solution)/shard_map/scatter_pack/pallas_call | solution.py:327
  144.9 0.0 reduce-scatter.2.cloned.1.call-update
  144.9 5.5 %all-to-all-start.2 = ((bf16[8,288,256]{2,1,0:T(8,128)(2,1)}), bf16[8,288,256]{2,1,0:T(8,128)(2,1)S(1)}, u32[]{:S(2)}, u32[]{:S(2)}) async-start(bf16[8,288,256]{2,1,0:T(8,128)(2,1)} %copy-done.6), calls=%async_computation.2 | async-start | bytes 2359296 | tf_op jit(solution)/shard_map/all_to_all | solution.py:344
  150.4 41.6 %reduce-scatter.2.cloned.1.call-done.x_ref = bf16[24,1280]{1,0:T(8,128)(2,1)} async-done(((bf16[96,1280]{1,0:T(8,128)(2,1)}), bf16[24,1280]{1,0:T(8,128)(2,1)}) %reduce-scatter.2.cloned.1.call-update) | async-done | bytes 61456 | tf_op jit(solution)/shard_map/reduce_scatter | solution.py:333
  192.1 0.0 copy-start.8
  192.1 0.8 copy-done.8
  192.9 0.7 finish.1
  193.6 0.0 all-to-all-done.2.g_ref
  193.6 1.4 unpack_grads.1
  (1 shorter events, 0.0 us)
Async XLA Ops:
  7.2 12.0 %copy-start = (bf16[72,1152]{1,0:T(8,128)(2,1)S(1)}, bf16[72,1152]{1,0:T(8,128)(2,1)}, u32[]{:S(2)}) copy-start(bf16[72,1152]{1,0:T(8,128)(2,1)} %param.9) | copy-start | bytes 497668
  7.2 11.0 %copy-start.7 = (bf16[1,256,1152]{2,1,0:T(8,128)(2,1)S(1)}, bf16[1,256,1152]{2,1,0:T(8,128)(2,1)}, u32[]{:S(2)}) copy-start(bf16[1,256,1152]{2,1,0:T(8,128)(2,1)} %param.7) | copy-start | bytes 1769476
  7.2 12.0 %copy-start.1 = (bf16[1,768,1152]{2,1,0:T(8,128)(2,1)S(1)}, bf16[1,768,1152]{2,1,0:T(8,128)(2,1)}, u32[]{:S(2)}) copy-start(bf16[1,768,1152]{2,1,0:T(8,128)(2,1)} %param.8) | copy-start | bytes 5308420
  9.6 42.1 %all-to-all-start = ((bf16[8,160,256]{2,1,0:T(8,128)(2,1)}), bf16[8,160,256]{2,1,0:T(8,128)(2,1)S(1)}, u32[]{:S(2)}, u32[]{:S(2)}) async-start(bf16[8,160,256]{2,1,0:T(8,128)(2,1)} %pack_keys.1), calls=%async_computation | async-start | bytes 1310720 | tf_op jit(solution)/shard_map/all_to_all | solution.py:255
  18.4 0.8 copy-start.2
  51.8 34.4 %all-to-all-start.1 = ((bf16[8,144,256]{2,1,0:T(8,128)(2,1)}), bf16[8,144,256]{2,1,0:T(8,128)(2,1)S(1)}, u32[]{:S(2)}, u32[]{:S(2)}) async-start(bf16[8,144,256]{2,1,0:T(8,128)(2,1)} %copy-done.2), calls=%async_computation.1 | async-start | bytes 1179648 | tf_op jit(solution)/shard_map/all_to_all | solution.py:269
  57.5 8.0 %collective-permute-start = (bf16[2,72,384]{2,1,0:T(8,128)(2,1)}, bf16[2,72,384]{2,1,0:T(8,128)(2,1)S(1)}, u32[]{:S(2)}, u32[]{:S(2)}) collective-permute-start(bf16[2,72,384]{2,1,0:T(8,128)(2,1)} %get-tuple-element.27), channel_id=1, source_target_pairs={{0,1},{1,0},{2,3},{3,2},{4,5},{5,4},{6,7},{7,6},{8,9},{9,8},{10,11... | collective-permute-start | bytes 331784 | tf_op jit(solution)/shard_map/ppermute | solution.py:272
  86.1 0.9 copy-start.3
  111.3 0.7 copy-start.5
  112.1 17.4 %all-to-all-start.4 = ((bf16[32,48,128]{2,1,0:T(8,128)(2,1)}), bf16[32,48,128]{2,1,0:T(8,128)(2,1)}, u32[]{:S(2)}, u32[]{:S(2)}) async-start(bf16[32,48,128]{2,1,0:T(8,128)(2,1)} %copy-done.5), calls=%async_computation.4 | async-start | bytes 786432 | tf_op jit(solution)/shard_map/all_to_all | solution.py:305
  119.0 73.0 %reduce-scatter.2.cloned.1.call-start = ((), (), s32[]{:S(2)}) async-start(), calls=%async_computation.6 | async-start | bytes 307200 | tf_op jit(solution)/shard_map/reduce_scatter | solution.py:333
  119.2 0.9 copy-start.4
  128.1 1.0 copy-start.6
  144.9 48.7 %all-to-all-start.2 = ((bf16[8,288,256]{2,1,0:T(8,128)(2,1)}), bf16[8,288,256]{2,1,0:T(8,128)(2,1)S(1)}, u32[]{:S(2)}, u32[]{:S(2)}) async-start(bf16[8,288,256]{2,1,0:T(8,128)(2,1)} %copy-done.6), calls=%async_computation.2 | async-start | bytes 2359296 | tf_op jit(solution)/shard_map/all_to_all | solution.py:344
  192.1 0.8 copy-start.8
Sparse Core Ops, SparseCore 0:
  145.0 46.9 reduce-scatter.1

commit v6 on v5

--- a/solution.py
+++ b/solution.py
@@ -15,7 +15,6 @@
 BF = jnp.bfloat16
 F32 = jnp.float32
 VMEM = 24 * 1024 * 1024
-LONG = pl.CostEstimate(flops=60_000_000_000, bytes_accessed=200_000_000, transcendentals=0)
 ANY = pl.BlockSpec(memory_space=pl.ANY)
 SCALAR = pl.BlockSpec(memory_space=pltpu.SMEM)
 HERE = pl.BlockSpec(memory_space=pltpu.VMEM)
@@ -333,14 +332,6 @@
     summed = lax.psum_scatter(
         scattered.reshape(96, 1280), "t", scatter_dimension=0, tiled=True
     )
-    query_out, weight_out = pl.pallas_call(
-        finish_kernel,
-        out_shape=[jax.ShapeDtypeStruct((24, 1152), BF), jax.ShapeDtypeStruct((36, HD), F32)],
-        compiler_params=PARAMS,
-        cost_estimate=LONG,
-        name="finish",
-    )(summed)
-
     grads_back = lax.all_to_all(grads, CUBE, 0, 0, tiled=True)
     key_out, value_out = pl.pallas_call(
         unpack_kernel,
@@ -350,6 +341,13 @@
         compiler_params=PARAMS,
         name="unpack_grads",
     )(grads_back)
+    summed, key_out = lax.optimization_barrier((summed, key_out))
+    query_out, weight_out = pl.pallas_call(
+        finish_kernel,
+        out_shape=[jax.ShapeDtypeStruct((24, 1152), BF), jax.ShapeDtypeStruct((36, HD), F32)],
+        compiler_params=PARAMS,
+        name="finish",
+    )(summed)
     return (key_out[None], value_out[None], query_out[None], weight_out.T)
 
 

time: 203 us -> 201 us (level)
  waiting for transfers between devices: 46.6 us -> 44.2 us
    reduce_scatter x1, waiting for transfers between devices: 41.6 us -> 11.1 us  [on_device(): lax.psum_scatter(scattered.reshape(96, 1280), 't', scatter_dimension=0, t...]
    all_to_all x1, waiting for transfers between devices: 0.01 us -> 28.4 us  [on_device(): grads_back = lax.all_to_all(grads, CUBE, 0, 0, tiled=True)]
    unnamed x18 -> x20, local copies, waits for them, and re-layouts: 5.29 us -> 5.97 us
  transfers between devices with their start and end apart: 6 -> 6, of which waited for: 3 -> 3; matrix products, arithmetic and copies ran while one was open for 1% -> 1% of each run, Pallas kernels for 4% -> 6%
where the time goes in v6:
time: 201 us
  blocking collectives  82.6 us (41%)
  waiting for transfers between devices  44.2 us (22%)
  starting transfers between devices  29.8 us (15%)
  Pallas kernels  22 us (11%)
  between operations  14.2 us (7%)
  local copies, waits for them, and re-layouts  6.65 us (3%)
    all_gather x1, blocking collectives, on_device(): grad_four = lax.all_gather(grad_half, 't')  32.1 us
    all_to_all x1, waiting for transfers between devices, on_device(): grads_back = lax.all_to_all(grads, CUBE, 0, 0, tiled=True)  28.4 us
    all_gather x1, blocking collectives, on_device(): query_pieces = lax.all_gather(keys[:, 144:160, :].reshape(128, 256), 't')  19.8 us
    all_gather x1, blocking collectives, on_device(): gathered = lax.all_gather(stats, 't')  17.3 us
    all_to_all x1, blocking collectives, on_device(): query_come = lax.all_to_all(query_grad, CUBE, 0, 0, tiled=True)  13.3 us
    reduce_scatter x1, waiting for transfers between devices, on_device(): lax.psum_scatter(scattered.reshape(96, 1280), 't', scatter_dimension=0, t...  11.1 us
    all_to_all x1, starting transfers between devices, on_device(): keys = lax.all_to_all(packed_keys, CUBE, 0, 0, tiled=True)  8.49 us
    pallas_call x1, Pallas kernels, on_device(): pl.pallas_call(second_kernel, out_shape=[jax.ShapeDtypeStruct((8, 288, 25...  7.94 us
  transfers between devices with their start and end apart: 6, of which 3 were waited for; matrix products, arithmetic and copies ran while one was open for 1% of the time, Pallas kernels for 6%

profile of v6, /device:TPU:64, one launch (start us, length us, event | category | flops | bytes accessed | tf_op | source)
XLA Modules:
  0.0 200.5 jit_solution(3628818296581003906)
XLA Ops:
  7.2 0.0 copy-start
  7.2 0.0 copy-start.7
  7.2 0.0 copy-start.1
  7.2 2.4 %pack_keys.1 = bf16[8,160,256]{2,1,0:T(8,128)(2,1)} custom-call(s32[1]{0:T(128)} %bitcast.half_ref, bf16[256,1152]{1,0:T(8,128)(2,1)} %bitcast.27, bf16[48,1152]{1,0:T(8,128)(2,1)} %bitcast.29), custom_call_target="tpu_custom_call" | custom-call | tf_op jit(solution)/shard_map/pack_keys/pallas_call | solution.py:247
  9.6 8.5 %all-to-all-start = ((bf16[8,160,256]{2,1,0:T(8,128)(2,1)}), bf16[8,160,256]{2,1,0:T(8,128)(2,1)S(1)}, u32[]{:S(2)}, u32[]{:S(2)}) async-start(bf16[8,160,256]{2,1,0:T(8,128)(2,1)} %pack_keys.1), calls=%async_computation | async-start | bytes 1310720 | tf_op jit(solution)/shard_map/all_to_all | solution.py:254
  18.1 0.0 copy-done.7
  18.1 0.2 pack_values.1
  18.4 0.0 copy-start.2
  18.4 0.8 copy-done.2
  19.2 0.0 copy-done
  19.2 0.0 copy-done.1
  19.2 0.4 fusion
  19.6 32.1 %all-gather = bf16[288,384]{1,0:T(8,128)(2,1)S(1)} all-gather(bf16[72,384]{1,0:T(8,128)(2,1)S(1)} %fusion), channel_id=2, replica_groups=mesh['y'=4,'xh'=2,'core'=2,'t'=4,'j'=4,'kv'=2] {'t'}, dimensions={0}, use_global_device_ids=true | all-gather | bytes 276480 | tf_op jit(solution)/shard_map/all_gather | solution.py:266
  51.8 0.0 all-to-all-done.k_ref
  51.8 5.1 %all-to-all-start.1 = ((bf16[8,144,256]{2,1,0:T(8,128)(2,1)}), bf16[8,144,256]{2,1,0:T(8,128)(2,1)S(1)}, u32[]{:S(2)}, u32[]{:S(2)}) async-start(bf16[8,144,256]{2,1,0:T(8,128)(2,1)} %copy-done.2), calls=%async_computation.1 | async-start | bytes 1179648 | tf_op jit(solution)/shard_map/all_to_all | solution.py:268
  56.9 0.7 constant_dynamic-slice_fusion.1
  57.5 3.4 %collective-permute-start = (bf16[2,72,384]{2,1,0:T(8,128)(2,1)}, bf16[2,72,384]{2,1,0:T(8,128)(2,1)S(1)}, u32[]{:S(2)}, u32[]{:S(2)}) collective-permute-start(bf16[2,72,384]{2,1,0:T(8,128)(2,1)} %get-tuple-element.31), channel_id=1, source_target_pairs={{0,1},{1,0},{2,3},{3,2},{4,5},{5,4},{6,7},{7,6},{8,9},{9,8},{10,11... | collective-permute-start | bytes 331784 | tf_op jit(solution)/shard_map/ppermute | solution.py:271
  60.9 4.6 %collective-permute-done = bf16[2,72,384]{2,1,0:T(8,128)(2,1)S(1)} collective-permute-done((bf16[2,72,384]{2,1,0:T(8,128)(2,1)}, bf16[2,72,384]{2,1,0:T(8,128)(2,1)S(1)}, u32[]{:S(2)}, u32[]{:S(2)}) %collective-permute-start) | collective-permute-done | bytes 110624 | tf_op jit(solution)/shard_map/ppermute | solution.py:271
  65.5 0.7 maximum_select_fusion.ga_ref
  66.3 19.8 %all_gather.17 = bf16[4,128,256]{2,1,0:T(8,128)(2,1)S(1)} all-gather(bf16[1,128,256]{2,1,0:T(8,128)(2,1)S(1)} %bitcast.28), channel_id=1, replica_groups=mesh['y'=4,'xh'=2,'core'=2,'t'=4,'j'=4,'kv'=2] {'t'}, dimensions={0}, use_global_device_ids=true | all-gather | bytes 327680 | tf_op jit(solution)/shard_map/all_gather | solution.py:273
  86.1 0.0 all-to-all-done.1.v_ref
  86.1 0.0 copy-start.3
  86.1 0.9 copy-done.3
  87.0 6.1 %first_pass.1 = (f32[8,768]{1,0:T(8,128)S(1)}, f32[2,72,768]{2,1,0:T(8,128)S(1)}) custom-call(bf16[8,160,256]{2,1,0:T(8,128)(2,1)S(1)} %all-to-all-done.k_ref, bf16[8,144,256]{2,1,0:T(8,128)(2,1)S(1)} %all-to-all-done.1.v_ref, bf16[32,16,256]{2,1,0:T(8,128)(2,1)S(1)} %bitcast.21, bf16[2,72,768]{2,1,0:T(8,128)(2,1)S(1)} %copy-done.3), custom_call_target="tpu_custom_call" | custom-call | tf_op jit(solution)/shard_map/first_pass/pallas_call | solution.py:281
  93.2 17.3 %all-gather.1 = f32[32,768]{1,0:T(8,128)S(1)} all-gather(f32[8,768]{1,0:T(8,128)S(1)} %get-tuple-element.19.st_ref), channel_id=3, replica_groups=mesh['y'=4,'xh'=2,'core'=2,'t'=4,'j'=4,'kv'=2] {'t'}, dimensions={0}, use_global_device_ids=true | all-gather | bytes 122880 | tf_op jit(solution)/shard_map/all_gather | solution.py:296
  110.5 0.7 weight_part.1
  111.2 0.0 copy-start.5
  111.2 0.7 copy-done.5
  112.0 7.3 %all-to-all-start.3 = ((bf16[32,48,128]{2,1,0:T(8,128)(2,1)}), bf16[32,48,128]{2,1,0:T(8,128)(2,1)}, u32[]{:S(2)}, u32[]{:S(2)}) async-start(bf16[32,48,128]{2,1,0:T(8,128)(2,1)} %copy-done.5), calls=%async_computation.3 | async-start | bytes 786432 | tf_op jit(solution)/shard_map/all_to_all | solution.py:304
  119.3 0.0 copy-start.4
  119.3 0.9 copy-done.4
  120.2 7.9 %second_pass.1 = (bf16[8,288,256]{2,1,0:T(8,128)(2,1)S(1)}, bf16[8,112,128]{2,1,0:T(8,128)(2,1)S(1)}) custom-call(bf16[8,160,256]{2,1,0:T(8,128)(2,1)S(1)} %all-to-all-done.k_ref, bf16[8,144,256]{2,1,0:T(8,128)(2,1)S(1)} %all-to-all-done.1.v_ref, bf16[32,16,256]{2,1,0:T(8,128)(2,1)S(1)} %bitcast.22, bf16[2,72,768]{2,1,0:T(8,128)(2,1)S(1)} %copy-done.4, ...), custom_call_target="tpu_custom_call" | custom-call | tf_op jit(solution)/shard_map/second_pass/pallas_call | solution.py:307
  128.2 0.0 copy-start.6
  128.2 1.0 copy-done.6
  129.2 0.0 copy-start.8
  129.2 0.7 copy-done.8
  129.9 0.0 all-to-all-done.3.w_ref
  129.9 13.3 %all_to_all.25.g_ref = bf16[8,112,128]{2,1,0:T(8,128)(2,1)S(1)} all-to-all(bf16[8,112,128]{2,1,0:T(8,128)(2,1)} %copy-done.8), channel_id=1, replica_groups=mesh['y'=4,'xh'=2,'core'=2,'t'=4,'j'=4,'kv'=2] {'j','kv'}, dimensions={0} | all-to-all | bytes 458752 | tf_op jit(solution)/shard_map/all_to_all | solution.py:325
  143.2 5.5 %all-to-all-start.4 = ((bf16[8,288,256]{2,1,0:T(8,128)(2,1)}), bf16[8,288,256]{2,1,0:T(8,128)(2,1)S(1)}, u32[]{:S(2)}, u32[]{:S(2)}) async-start(bf16[8,288,256]{2,1,0:T(8,128)(2,1)} %copy-done.6), calls=%async_computation.5 | async-start | bytes 2359296 | tf_op jit(solution)/shard_map/all_to_all | solution.py:335
  148.8 0.0 reduce-scatter.2.cloned.1.call-start
  148.8 2.3 %scatter_pack.1 = bf16[4,24,1280]{2,1,0:T(8,128)(2,1)} custom-call(bf16[8,112,128]{2,1,0:T(8,128)(2,1)S(1)} %all_to_all.25.g_ref, bf16[32,48,128]{2,1,0:T(8,128)(2,1)} %all-to-all-done.3.w_ref), custom_call_target="tpu_custom_call" | custom-call | tf_op jit(solution)/shard_map/scatter_pack/pallas_call | solution.py:326
  151.1 0.0 reduce-scatter.2.cloned.1.call-update
  151.1 28.4 %all-to-all-done.4.g_ref = bf16[8,288,256]{2,1,0:T(8,128)(2,1)S(1)} async-done(((bf16[8,288,256]{2,1,0:T(8,128)(2,1)}), bf16[8,288,256]{2,1,0:T(8,128)(2,1)S(1)}, u32[]{:S(2)}, u32[]{:S(2)}) %all-to-all-start.4) | async-done | bytes 1179680 | tf_op jit(solution)/shard_map/all_to_all | solution.py:335
  179.6 1.4 unpack_grads.1
  181.0 11.1 %reduce-scatter.2.cloned.1.call-done.x_ref = bf16[24,1280]{1,0:T(8,128)(2,1)} async-done(((bf16[96,1280]{1,0:T(8,128)(2,1)}), bf16[24,1280]{1,0:T(8,128)(2,1)}) %reduce-scatter.2.cloned.1.call-update) | async-done | bytes 61456 | tf_op jit(solution)/shard_map/reduce_scatter | solution.py:332
  192.1 0.0 copy-start.9
  192.1 0.8 copy-done.9
  192.9 0.7 finish.1
  (1 shorter events, 0.0 us)
Async XLA Ops:
  7.2 12.0 %copy-start = (bf16[72,1152]{1,0:T(8,128)(2,1)S(1)}, bf16[72,1152]{1,0:T(8,128)(2,1)}, u32[]{:S(2)}) copy-start(bf16[72,1152]{1,0:T(8,128)(2,1)} %param.9) | copy-start | bytes 497668
  7.2 10.9 %copy-start.7 = (bf16[1,256,1152]{2,1,0:T(8,128)(2,1)S(1)}, bf16[1,256,1152]{2,1,0:T(8,128)(2,1)}, u32[]{:S(2)}) copy-start(bf16[1,256,1152]{2,1,0:T(8,128)(2,1)} %param.7) | copy-start | bytes 1769476
  7.2 12.0 %copy-start.1 = (bf16[1,768,1152]{2,1,0:T(8,128)(2,1)S(1)}, bf16[1,768,1152]{2,1,0:T(8,128)(2,1)}, u32[]{:S(2)}) copy-start(bf16[1,768,1152]{2,1,0:T(8,128)(2,1)} %param.8) | copy-start | bytes 5308420
  9.6 42.1 %all-to-all-start = ((bf16[8,160,256]{2,1,0:T(8,128)(2,1)}), bf16[8,160,256]{2,1,0:T(8,128)(2,1)S(1)}, u32[]{:S(2)}, u32[]{:S(2)}) async-start(bf16[8,160,256]{2,1,0:T(8,128)(2,1)} %pack_keys.1), calls=%async_computation | async-start | bytes 1310720 | tf_op jit(solution)/shard_map/all_to_all | solution.py:254
  18.4 0.8 copy-start.2
  51.8 34.3 %all-to-all-start.1 = ((bf16[8,144,256]{2,1,0:T(8,128)(2,1)}), bf16[8,144,256]{2,1,0:T(8,128)(2,1)S(1)}, u32[]{:S(2)}, u32[]{:S(2)}) async-start(bf16[8,144,256]{2,1,0:T(8,128)(2,1)} %copy-done.2), calls=%async_computation.1 | async-start | bytes 1179648 | tf_op jit(solution)/shard_map/all_to_all | solution.py:268
  57.5 8.0 %collective-permute-start = (bf16[2,72,384]{2,1,0:T(8,128)(2,1)}, bf16[2,72,384]{2,1,0:T(8,128)(2,1)S(1)}, u32[]{:S(2)}, u32[]{:S(2)}) collective-permute-start(bf16[2,72,384]{2,1,0:T(8,128)(2,1)} %get-tuple-element.31), channel_id=1, source_target_pairs={{0,1},{1,0},{2,3},{3,2},{4,5},{5,4},{6,7},{7,6},{8,9},{9,8},{10,11... | collective-permute-start | bytes 331784 | tf_op jit(solution)/shard_map/ppermute | solution.py:271
  86.1 0.9 copy-start.3
  111.2 0.7 copy-start.5
  112.0 17.9 %all-to-all-start.3 = ((bf16[32,48,128]{2,1,0:T(8,128)(2,1)}), bf16[32,48,128]{2,1,0:T(8,128)(2,1)}, u32[]{:S(2)}, u32[]{:S(2)}) async-start(bf16[32,48,128]{2,1,0:T(8,128)(2,1)} %copy-done.5), calls=%async_computation.3 | async-start | bytes 786432 | tf_op jit(solution)/shard_map/all_to_all | solution.py:304
  119.3 0.9 copy-start.4
  128.2 1.0 copy-start.6
  129.2 0.7 copy-start.8
  143.2 36.3 %all-to-all-start.4 = ((bf16[8,288,256]{2,1,0:T(8,128)(2,1)}), bf16[8,288,256]{2,1,0:T(8,128)(2,1)S(1)}, u32[]{:S(2)}, u32[]{:S(2)}) async-start(bf16[8,288,256]{2,1,0:T(8,128)(2,1)} %copy-done.6), calls=%async_computation.5 | async-start | bytes 2359296 | tf_op jit(solution)/shard_map/all_to_all | solution.py:335
  148.8 43.3 %reduce-scatter.2.cloned.1.call-start = ((), (), s32[]{:S(2)}) async-start(), calls=%async_computation.6 | async-start | bytes 307200 | tf_op jit(solution)/shard_map/reduce_scatter | solution.py:332
  192.1 0.8 copy-start.9
Sparse Core Ops, SparseCore 0:
  152.4 39.6 reduce-scatter.1
